TPU v7x, 768 devices: a whole 4x8x12 slice. The times are simulated.
768 devices in a mesh: slab: 96 (over y, z), cut: 8 (over x, core).
Axes of the slice: x: 4, y: 8, z: 12, core: 2. Of those that a mesh axis runs over, the one named last changes fastest.
Arguments:
- conserved: float32 [5, 512, 98304], P(None, None, ('slab', 'cut')), may hold values from -2 to 21, as said below
- refinement: int32 [98304], P(('slab', 'cut')), may hold values from 0 to 2
- x_neighbour: int32 [768, 128], P(('slab', 'cut')), may hold values from 0 to 127, each once within a row
- coarse_element: int32 [96, 8, 4, 32], P('slab', 'cut'), may hold values from 0 to 127, as said below
- quadrant: int32 [96, 8, 4, 32], P('slab', 'cut'), may hold values from 0 to 3, as said below
- send_count: int32 [96, 8, 4], P('slab', 'cut'), may hold values from 8 to 32, as said below
- fine_element: int32 [96, 8, 4, 32], P('slab', 'cut'), may hold values from 0 to 127, as said below
- orientation: int32 [96, 8, 4, 32], P('slab', 'cut'), may hold values from 0 to 3
- receive_count: int32 [96, 8, 4], P('slab', 'cut'), may hold values from 8 to 32, as said below
Outputs:
- advanced: float32 [5, 512, 98304], P(None, None, ('slab', 'cut'))
- register: float32 [5, 512, 98304], P(None, None, ('slab', 'cut'))
Inputs may be any that keep to these rules, and one draw needn't show every extreme that they name: `conserved`: density lies in 0.6 to 1.4 and pressure is positive at every node. `coarse_element`: slots j and j2 of one device and offset with j // 4 == j2 // 4 name the same element, and no element is named in two such groups of a device. `quadrant`: within each group of 4 slots (j // 4 equal) the sub-faces 0 to 3 appear once each; sub-face q covers half q // 2 along a and half q % 2 along c. `send_count`: for every offset some device sends 32 live links. `fine_element`: no element is named twice on one device. receive_count[s, t, o] equals send_count[(s - k_o) mod 96, t, o].
All inputs are finite; a program needn't handle non-finite values.
Results may differ from a plain program's by a relative error of at most 0.0003.
Values sent between devices are 32-bit elements; how exact they have to be, the bound alone decides.
A program may use at most 128 MiB of HBM per device.

v0:
```python
import jax
import jax.numpy as jnp
import numpy as np
from jax import lax
from jax.sharding import PartitionSpec as P

NP = 8
NVAR = 5


gamma_ratio = 1.4
courant = 0.005
section_a = (0.0, -567301805773.0 / 1357537059087.0)
section_b = (1432997174477.0 / 9575080441755.0, 5161836677717.0 / 13612068292357.0)


def passed_along(block, axis, distance):
    devices = range(lax.axis_size(axis))
    route = [((i - distance) % len(devices), i) for i in devices]
    return lax.ppermute(block, axis, route)


def extended(block, sides, width):
    for axis, dim in sides:
        count = lax.axis_size(axis)
        forward = [(i, i + 1) for i in range(count - 1)]
        forward.append((count - 1, 0))
        backward = [(target, source) for source, target in forward]
        low = lax.ppermute(
            lax.slice_in_dim(block, block.shape[dim] - width, None, axis=dim), axis, forward
        )
        high = lax.ppermute(lax.slice_in_dim(block, 0, width, axis=dim), axis, backward)
        block = jnp.concatenate([low, block, high], axis=dim)
    return block


def legendre_rows(points, node_count):
    legendre = np.zeros((node_count, node_count))
    legendre[:, 0] = 1.0
    legendre[:, 1] = points
    for degree in range(2, node_count):
        legendre[:, degree] = (
            (2 * degree - 1) * points * legendre[:, degree - 1]
            - (degree - 1) * legendre[:, degree - 2]
        ) / degree
    return legendre


def lobatto(node_count):
    poly_order = node_count - 1
    points = -np.cos(np.pi * np.arange(node_count) / poly_order)
    for newton_step in range(40):
        legendre = legendre_rows(points, node_count)
        points = points - (points * legendre[:, poly_order] - legendre[:, poly_order - 1]) / (
            node_count * legendre[:, poly_order]
        )
    top_row = legendre_rows(points, node_count)[:, poly_order]
    weights = 2.0 / (poly_order * node_count * top_row * top_row)
    differ = np.zeros((node_count, node_count))
    for target in range(node_count):
        for source in range(node_count):
            if target != source:
                differ[target, source] = top_row[target] / (
                    top_row[source] * (points[target] - points[source])
                )
    differ[0, 0] = -poly_order * node_count / 4.0
    differ[poly_order, poly_order] = poly_order * node_count / 4.0
    to_half = np.zeros((2, node_count, node_count))
    for half_side in range(2):
        targets = (points + 2 * half_side - 1) / 2.0
        for source in range(node_count):
            basis = np.ones(node_count)
            for other in range(node_count):
                if other != source:
                    basis = basis * (targets - points[other]) / (points[source] - points[other])
            to_half[half_side, :, source] = basis
    from_half = (
        0.5 * np.transpose(to_half, (0, 2, 1)) * weights[None, None, :] / weights[None, :, None]
    )
    return (weights, differ, to_half, from_half)


def make_tables():
    return tuple((jnp.asarray(table, dtype=jnp.float32) for table in lobatto(NP)))


def level_metric(refinement):
    return jnp.where(refinement == 0, 1.0, jnp.where(refinement == 1, 2.0, 4.0)).astype(jnp.float32)


def offset_distance(offset_index):
    return (offset_index // 2 + 1) * (1 - 2 * (offset_index % 2))


def primitives(state):
    density = state[0]
    velocity = state[1:4] / density
    pressure = (gamma_ratio - 1.0) * (state[4] - 0.5 * jnp.sum(state[1:4] * velocity, axis=0))
    return (density, velocity, pressure)


def directional_flux(state, velocity, pressure, direction):
    normal_speed = velocity[direction]
    flux_rows = [state[1 + direction]]
    for column in range(3):
        carried = state[1 + column] * normal_speed
        flux_rows.append(carried + pressure if column == direction else carried)
    flux_rows.append(normal_speed * (state[4] + pressure))
    return jnp.stack(flux_rows)


def face_flux(state, direction):
    density, velocity, pressure = primitives(state)
    sound_speed = jnp.sqrt(gamma_ratio * pressure / density)
    return (
        directional_flux(state, velocity, pressure, direction),
        jnp.abs(velocity[direction]) + sound_speed,
    )


def numerical_flux(left_state, right_state, direction):
    left_flux, left_speed = face_flux(left_state, direction)
    right_flux, right_speed = face_flux(right_state, direction)
    fastest = jnp.maximum(left_speed, right_speed)
    flux_star = 0.5 * (left_flux + right_flux) - 0.5 * fastest * (right_state - left_state)
    return (flux_star, left_flux, right_flux)


def wave_speed(state5, metric):
    density, velocity, pressure = primitives(state5)
    return metric * (
        jnp.sqrt(jnp.sum(velocity * velocity, axis=0)) + jnp.sqrt(gamma_ratio * pressure / density)
    )


def sub_face(values, quadrant, matrices):
    highest = lax.Precision.HIGHEST
    along_a = [
        jnp.einsum("ia,vac...->vic...", matrices[half_side], values, precision=highest)
        for half_side in range(2)
    ]
    chosen = jnp.where(quadrant // 2 == 1, along_a[1], along_a[0])
    along_c = [
        jnp.einsum("jc,vic...->vij...", matrices[half_side], chosen, precision=highest)
        for half_side in range(2)
    ]
    return jnp.where(quadrant % 2 == 1, along_c[1], along_c[0])


def rotate_turns(values, turns):
    options = [jnp.rot90(values, turn_count, axes=(1, 2)) for turn_count in range(4)]
    result = options[0]
    for turn_count in range(1, 4):
        result = jnp.where(turns == turn_count, options[turn_count], result)
    return result


def take_last(values, index):
    shaped = index.reshape((1,) * (values.ndim - index.ndim) + index.shape)
    return jnp.take_along_axis(values, shaped, axis=-1)


def derive_lifted(flux, axis, low_term, high_term, differ_table, lift_scale):
    rows = []
    for target in range(NP):
        total = float(differ_table[target, 0]) * lax.index_in_dim(flux, 0, axis, keepdims=False)
        for source in range(1, NP):
            total = total + float(differ_table[target, source]) * lax.index_in_dim(
                flux, source, axis, keepdims=False
            )
        if target == 0:
            total = total + lift_scale * low_term
        if target == NP - 1:
            total = total + lift_scale * high_term
        rows.append(total)
    return jnp.stack(rows, axis=axis)


def body_rate(
    state5,
    metric,
    neighbour,
    below_top,
    above_bottom,
    coarse_face,
    fine_face,
    lift_scale,
    differ_table,
):
    far_node = NP - 1
    density, velocity, pressure = primitives(state5)
    flux_star, left_flux, right_flux = numerical_flux(
        state5[:, far_node], take_last(state5[:, 0], neighbour), 0
    )
    x_plus = flux_star - left_flux
    x_minus = take_last(right_flux - flux_star, jnp.argsort(neighbour, axis=-1))
    flux_star, left_flux, right_flux = numerical_flux(state5[:, :, :, far_node], above_bottom, 2)
    z_plus = flux_star - left_flux
    flux_star, left_flux, right_flux = numerical_flux(below_top, state5[:, :, :, 0], 2)
    z_minus = right_flux - flux_star
    total = derive_lifted(
        directional_flux(state5, velocity, pressure, 0),
        1,
        x_minus,
        x_plus,
        differ_table,
        lift_scale,
    )
    total = total + derive_lifted(
        directional_flux(state5, velocity, pressure, 1),
        2,
        fine_face,
        coarse_face,
        differ_table,
        lift_scale,
    )
    total = total + derive_lifted(
        directional_flux(state5, velocity, pressure, 2),
        3,
        z_minus,
        z_plus,
        differ_table,
        lift_scale,
    )
    return -metric * total


def on_device(
    conserved,
    refinement,
    x_neighbour,
    coarse_element,
    quadrant,
    send_count,
    fine_element,
    orientation,
    receive_count,
):
    tables = make_tables()
    weights, differ, to_half, from_half = tables
    weights_np, differ_np, half_np, back_np = lobatto(NP)
    differ_table = np.asarray(differ_np, dtype=np.float32)
    lift_scale = 1.0 / weights[0]
    highest = lax.Precision.HIGHEST
    element_count = conserved.shape[2]
    offsets = coarse_element.shape[2]
    slot_count = coarse_element.shape[3]
    far_node = NP - 1
    metric = level_metric(refinement)
    neighbour = x_neighbour.reshape(-1)
    coarse_index = coarse_element.reshape(-1)
    coarse_quadrant = quadrant.reshape(-1)
    fine_index = fine_element.reshape(-1)
    fine_turns = orientation.reshape(-1)
    slot_ids = jnp.arange(slot_count)[None, :]
    coarse_live = (slot_ids < send_count.reshape(offsets, 1)).reshape(-1)
    fine_live = (slot_ids < receive_count.reshape(offsets, 1)).reshape(-1)
    element_ids = jnp.arange(element_count)[None, :]
    coarse_table = (coarse_index[:, None] == element_ids).astype(jnp.float32)
    fine_table = (fine_index[:, None] == element_ids).astype(jnp.float32)

    def mortar_terms(current):
        coarse_trace = jnp.take(current[:, :, far_node], coarse_index, axis=3)
        mortar_coarse = sub_face(coarse_trace, coarse_quadrant, to_half)
        fine_trace = jnp.take(current[:, :, 0], fine_index, axis=3)
        mortar_fine = rotate_turns(fine_trace, (4 - fine_turns) % 4)
        arrived = []
        for offset_index in range(offsets):
            lower = offset_index * slot_count
            arrived.append(
                passed_along(
                    mortar_coarse[..., lower : lower + slot_count],
                    "slab",
                    offset_distance(offset_index),
                )
            )
        received_coarse = jnp.concatenate(arrived, axis=3)
        flux_star, left_flux, right_flux = numerical_flux(received_coarse, mortar_fine, 1)
        fine_term = right_flux - flux_star
        coarse_share = flux_star - left_flux
        returned = []
        for offset_index in range(offsets):
            lower = offset_index * slot_count
            returned.append(
                passed_along(
                    coarse_share[..., lower : lower + slot_count],
                    "slab",
                    -offset_distance(offset_index),
                )
            )
        coarse_term = jnp.concatenate(returned, axis=3)
        coarse_values = jnp.where(
            coarse_live, sub_face(coarse_term, coarse_quadrant, from_half), 0.0
        )
        fine_values = jnp.where(fine_live, rotate_turns(fine_term, fine_turns), 0.0)
        coarse_face = jnp.einsum("vacl,le->vace", coarse_values, coarse_table, precision=highest)
        fine_face = jnp.einsum("vacl,le->vace", fine_values, fine_table, precision=highest)
        return (coarse_face, fine_face)

    def operate(current):
        stacked = jnp.stack([current[:, :, :, 0], current[:, :, :, far_node]])
        padded = extended(stacked, (("cut", 0),), 1)
        coarse_face, fine_face = mortar_terms(current)
        return body_rate(
            current,
            metric,
            neighbour,
            padded[0],
            padded[3],
            coarse_face,
            fine_face,
            lift_scale,
            differ_table,
        )

    state5 = conserved.reshape(NVAR, NP, NP, NP, element_count)
    fastest = lax.pmax(jnp.max(wave_speed(state5, metric)), ("slab", "cut"))
    step_size = courant / fastest
    register = step_size * operate(state5)
    sectioned = state5 + section_b[0] * register
    register = section_a[1] * register + step_size * operate(sectioned)
    advanced = sectioned + section_b[1] * register
    return (advanced.reshape(conserved.shape), register.reshape(conserved.shape))


def solution(mesh):
    return jax.shard_map(
        on_device,
        mesh=mesh,
        in_specs=(
            P(None, None, ("slab", "cut")),
            P(("slab", "cut")),
            P(("slab", "cut"), None),
            P("slab", "cut", None, None),
            P("slab", "cut", None, None),
            P("slab", "cut", None),
            P("slab", "cut", None, None),
            P("slab", "cut", None, None),
            P("slab", "cut", None),
        ),
        out_specs=(P(None, None, ("slab", "cut")), P(None, None, ("slab", "cut"))),
        check_vma=False,
    )
```

profile of v0, /device:TPU:1, one launch (start us, length us, event | category | flops | bytes accessed | tf_op | source)
XLA Modules:
  0.0 449.9 jit_solution(3056062343704824581)
XLA Ops:
  0.6 2.9 fusion.214
  4.2 2.6 collective-permute-start.8
  8.6 2.2 copy.1966
  11.5 4.2 gather_fusion.3
  15.7 3.5 select_bitcast_fusion.1
  19.3 2.5 copy.1700
  24.1 17.2 %collective-permute-start.3 = (f32[5,8,8,32]{3,1,2,0:T(8,128)}, f32[5,8,8,32]{3,1,2,0:T(8,128)}, u32[]{:S(2)}, u32[]{:S(2)}) collective-permute-start(f32[5,8,8,32]{3,1,2,0:T(8,128)} %get-tuple-element.210), channel_id=1, source_target_pairs={{16,0},{24,8},{32,16},{40,24},{48,32},{56,40},{64,48},{72,56},{80,... | collective-permute-start | bytes 122888 | tf_op jit(solution)/shard_map/ppermute | solution.py:20
  43.2 7.6 %collective-permute-start.1 = (f32[5,8,8,32]{3,1,2,0:T(8,128)}, f32[5,8,8,32]{3,1,2,0:T(8,128)}, u32[]{:S(2)}, u32[]{:S(2)}) collective-permute-start(f32[5,8,8,32]{3,1,2,0:T(8,128)} %get-tuple-element.212), channel_id=1, source_target_pairs={{8,0},{16,8},{24,16},{32,24},{40,32},{48,40},{56,48},{64,56},{72,6... | collective-permute-start | bytes 122888 | tf_op jit(solution)/shard_map/ppermute | solution.py:20
  57.4 2.5 sort.19
  71.1 4.3 gather_fusion.2
  75.4 2.5 copy.1696
  81.1 8.2 %add_add_fusion.1 = (f32[5,8,1,8,128]{4,2,0,1,3:T(1,128)}, f32[5,8,1,8,128]{4,2,0,1,3:T(1,128)}) fusion(f32[5,8,8,8,128]{4,2,0,1,3:T(8,128)} %copy-done.4), kind=kLoop, calls=%fused_computation.344 | loop fusion | flops 1228800 | bytes 1638400 | tf_op jit(solution)/shard_map/add | solution.py:168
  89.3 2.6 multiply_add_fusion.17
  91.9 2.6 multiply_add_fusion.18
  94.5 2.8 multiply_add_fusion.19
  103.0 4.2 gather_fusion
  107.2 2.5 copy.1657
  112.6 2.3 copy.1671
  114.9 4.1 gather_fusion.1
  119.0 3.1 copy.1672
  132.2 108.0 %pmax.7 = f32[]{:T(128)} all-reduce(f32[]{:T(128)} %get-tuple-element.179), channel_id=1, replica_groups=mesh['slab'=96,'cut'=8] {'slab','cut'}, use_global_device_ids=true, to_apply=%region_3.4 | all-reduce | flops 1 | bytes 8 | tf_op jit(solution)/shard_map/pmax | solution.py:317
  250.7 7.6 %collective-permute-start.6 = (f32[5,8,8,32]{3,1,2,0:T(8,128)S(1)}, f32[5,8,8,32]{3,1,2,0:T(8,128)S(1)}, u32[]{:S(2)}, u32[]{:S(2)}) collective-permute-start(f32[5,8,8,32]{3,1,2,0:T(8,128)S(1)} %get-tuple-element.203), channel_id=1, source_target_pairs={{16,0},{24,8},{32,16},{40,24},{48,32},{56,40},{64,48},{72,56},{80,... | collective-permute-start | bytes 122888 | tf_op jit(solution)/shard_map/ppermute | solution.py:20
  260.2 6.7 %collective-permute-start.4 = (f32[5,8,8,32]{3,1,2,0:T(8,128)S(1)}, f32[5,8,8,32]{3,1,2,0:T(8,128)S(1)}, u32[]{:S(2)}, u32[]{:S(2)}) collective-permute-start(f32[5,8,8,32]{3,1,2,0:T(8,128)S(1)} %get-tuple-element.201), channel_id=1, source_target_pairs={{8,0},{16,8},{24,16},{32,24},{40,32},{48,40},{56,48},{64,56},{72,6... | collective-permute-start | bytes 122888 | tf_op jit(solution)/shard_map/ppermute | solution.py:20
  272.0 5.0 %stack.155 = f32[5,8,8,8,128]{4,2,0,1,3:T(8,128)} concatenate(f32[5,8,1,8,128]{4,2,0,1,3:T(1,128)} %copy.1727, f32[5,8,1,8,128]{4,2,0,1,3:T(1,128)} %get-tuple-element.102, f32[5,8,1,8,128]{4,2,0,1,3:T(1,128)} %get-tuple-element.104, f32[5,8,1,8,128]{4,2,0,1,3:T(1,128)} %get-tuple-element.106, f32[5,8,1,8,128]{4,2,0,1,3:T(1,128)} %get-tuple-element.105, ...), dimensions={2} | concatenate | bytes 2621440 | tf_op jit(solution)/shard_map/stack | solution.py:176
  287.6 2.7 multiply_multiply_fusion
  300.2 2.3 copy.1865
  302.5 4.2 gather_fusion.7
  306.7 3.5 select_bitcast_fusion
  310.2 2.4 copy.1866
  314.5 2.2 copy.1861
  316.7 4.3 gather_fusion.6
  321.0 2.4 copy.1862
  324.8 8.5 %add_add_fusion = (f32[5,8,1,8,128]{4,2,0,1,3:T(1,128)}, f32[5,8,1,8,128]{4,2,0,1,3:T(1,128)}, f32[5,8,1,8,128]{4,2,0,1,3:T(1,128)}, f32[5,8,1,8,128]{4,2,0,1,3:T(1,128)}, f32[5,8,1,8,128]{4,2,0,1,3:T(1,128)}) fusion(f32[5,8,8,8,128]{4,2,0,1,3:T(8,128)} %copy-done.6), kind=kLoop, calls=%fused_computation.343 | loop fusion | flops 1351680 | bytes 2129920 | tf_op jit(solution)/shard_map/add | solution.py:168
  333.4 3.6 multiply_add_fusion.11
  336.9 3.2 multiply_add_fusion.12
  353.9 3.6 collective-permute-start.13
  357.5 2.6 collective-permute-start.12
  360.1 10.7 %collective-permute-start.11 = (f32[5,8,8,32]{3,1,2,0:T(8,128)}, f32[5,8,8,32]{3,1,2,0:T(8,128)}, u32[]{:S(2)}, u32[]{:S(2)}) collective-permute-start(f32[5,8,8,32]{3,1,2,0:T(8,128)} %get-tuple-element.196), channel_id=1, source_target_pairs={{8,0},{16,8},{24,16},{32,24},{40,32},{48,40},{56,48},{64,56},{72,6... | collective-permute-start | bytes 122888 | tf_op jit(solution)/shard_map/ppermute | solution.py:20
  375.7 3.1 copy.1824
  378.9 4.3 gather_fusion.4
  383.1 2.4 copy.1825
  389.0 3.1 copy.1833
  392.1 4.3 gather_fusion.5
  396.4 3.1 copy.1834
  411.7 7.6 %collective-permute-start.16 = (f32[5,8,8,32]{3,1,2,0:T(8,128)S(1)}, f32[5,8,8,32]{3,1,2,0:T(8,128)S(1)}, u32[]{:S(2)}, u32[]{:S(2)}) collective-permute-start(f32[5,8,8,32]{3,1,2,0:T(8,128)S(1)} %get-tuple-element.189), channel_id=1, source_target_pairs={{16,0},{24,8},{32,16},{40,24},{48,32},{56,40},{64,48},{72,56},{80,... | collective-permute-start | bytes 122888 | tf_op jit(solution)/shard_map/ppermute | solution.py:20
  421.5 6.5 %collective-permute-start.14 = (f32[5,8,8,32]{3,1,2,0:T(8,128)S(1)}, f32[5,8,8,32]{3,1,2,0:T(8,128)S(1)}, u32[]{:S(2)}, u32[]{:S(2)}) collective-permute-start(f32[5,8,8,32]{3,1,2,0:T(8,128)S(1)} %get-tuple-element.187), channel_id=1, source_target_pairs={{8,0},{16,8},{24,16},{32,24},{40,32},{48,40},{56,48},{64,56},{72,6... | collective-permute-start | bytes 122888 | tf_op jit(solution)/shard_map/ppermute | solution.py:20
  434.9 3.3 collective-permute-start.18
  440.8 3.5 stack.379
  (694 shorter events, 135.8 us)
Async XLA Ops:
  4.2 272.7 %collective-permute-start.8 = (f32[1,5,8,8,128]{4,3,1,2,0:T(8,128)}, f32[1,5,8,8,128]{4,3,1,2,0:T(8,128)}, u32[]{:S(2)}, u32[]{:S(2)}) collective-permute-start(f32[1,5,8,8,128]{4,3,1,2,0:T(8,128)} %bitcast.1338), channel_id=1, source_target_pairs={{0,1},{1,2},{2,3},{3,4},{4,5},{5,6},{6,7},{7,0},{8,9},{9,10},{10,1... | collective-permute-start | bytes 491528 | tf_op jit(solution)/shard_map/ppermute | solution.py:29
  22.5 30.5 %copy-start = (f32[5,512,128]{2,1,0:T(8,128)S(1)}, f32[5,512,128]{2,1,0:T(8,128)}, u32[]{:S(2)}) copy-start(f32[5,512,128]{2,1,0:T(8,128)} %param.16) | copy-start | bytes 3932164
  24.1 220.6 %collective-permute-start.3 = (f32[5,8,8,32]{3,1,2,0:T(8,128)}, f32[5,8,8,32]{3,1,2,0:T(8,128)}, u32[]{:S(2)}, u32[]{:S(2)}) collective-permute-start(f32[5,8,8,32]{3,1,2,0:T(8,128)} %get-tuple-element.210), channel_id=1, source_target_pairs={{16,0},{24,8},{32,16},{40,24},{48,32},{56,40},{64,48},{72,56},{80,... | collective-permute-start | bytes 122888 | tf_op jit(solution)/shard_map/ppermute | solution.py:20
  41.3 203.4 %collective-permute-start.2 = (f32[5,8,8,32]{3,1,2,0:T(8,128)}, f32[5,8,8,32]{3,1,2,0:T(8,128)}, u32[]{:S(2)}, u32[]{:S(2)}) collective-permute-start(f32[5,8,8,32]{3,1,2,0:T(8,128)} %get-tuple-element.211), channel_id=1, source_target_pairs={{752,0},{760,8},{0,16},{8,24},{16,32},{24,40},{32,48},{40,56},{48,... | collective-permute-start | bytes 122888 | tf_op jit(solution)/shard_map/ppermute | solution.py:20
  43.2 201.5 %collective-permute-start.1 = (f32[5,8,8,32]{3,1,2,0:T(8,128)}, f32[5,8,8,32]{3,1,2,0:T(8,128)}, u32[]{:S(2)}, u32[]{:S(2)}) collective-permute-start(f32[5,8,8,32]{3,1,2,0:T(8,128)} %get-tuple-element.212), channel_id=1, source_target_pairs={{8,0},{16,8},{24,16},{32,24},{40,32},{48,40},{56,48},{64,56},{72,6... | collective-permute-start | bytes 122888 | tf_op jit(solution)/shard_map/ppermute | solution.py:20
  50.8 193.9 %collective-permute-start = (f32[5,8,8,32]{3,1,2,0:T(8,128)}, f32[5,8,8,32]{3,1,2,0:T(8,128)}, u32[]{:S(2)}, u32[]{:S(2)}) collective-permute-start(f32[5,8,8,32]{3,1,2,0:T(8,128)} %get-tuple-element.209), channel_id=1, source_target_pairs={{760,0},{0,8},{8,16},{16,24},{24,32},{32,40},{40,48},{48,56},{56,6... | collective-permute-start | bytes 122888 | tf_op jit(solution)/shard_map/ppermute | solution.py:20
  56.1 55.7 %copy-start.137 = (pred[128]{0:T(512)(128)(4,1)}, pred[128]{0:T(512)(128)(4,1)S(1)}, u32[]{:S(2)}) copy-start(pred[128]{0:T(512)(128)(4,1)S(1)} %and_bitcast_fusion.1) | copy-start | bytes 388
  127.3 112.9 %copy-start.21 = (f32[5,8,8,1,128]{4,3,2,1,0:T(1,128)S(1)}, f32[5,8,8,1,128]{4,3,2,1,0:T(1,128)}, u32[]{:S(2)}) copy-start(f32[5,8,8,1,128]{4,3,2,1,0:T(1,128)} %get-tuple-element.142) | copy-start | bytes 491524
  128.0 113.0 %copy-start.180 = (pred[1,1,4,32]{3,2,1,0:T(4,128)(4,1)S(1)}, pred[1,1,4,32]{3,2,1,0:T(4,128)(4,1)}, u32[]{:S(2)}) copy-start(pred[1,1,4,32]{3,2,1,0:T(4,128)(4,1)} %get-tuple-element.233) | copy-start | bytes 388
  128.0 113.6 %copy-start.179 = (pred[1,1,4,32]{3,2,1,0:T(4,128)(4,1)S(1)}, pred[1,1,4,32]{3,2,1,0:T(4,128)(4,1)}, u32[]{:S(2)}) copy-start(pred[1,1,4,32]{3,2,1,0:T(4,128)(4,1)} %get-tuple-element.234) | copy-start | bytes 388
  128.0 114.2 %copy-start.178 = (pred[1,1,4,32]{3,2,1,0:T(4,128)(4,1)S(1)}, pred[1,1,4,32]{3,2,1,0:T(4,128)(4,1)}, u32[]{:S(2)}) copy-start(pred[1,1,4,32]{3,2,1,0:T(4,128)(4,1)} %get-tuple-element.232) | copy-start | bytes 388
  128.0 114.8 %copy-start.186 = (pred[4,32]{1,0:T(4,128)(4,1)S(1)}, pred[4,32]{1,0:T(4,128)(4,1)}, u32[]{:S(2)}) copy-start(pred[4,32]{1,0:T(4,128)(4,1)} %iota_compare_fusion.3) | copy-start | bytes 388
  130.7 115.5 %copy-start.112 = (f32[8,8,128]{2,0,1:T(8,128)S(1)}, f32[8,8,128]{2,0,1:T(8,128)}, u32[]{:S(2)}) copy-start(f32[8,8,128]{2,0,1:T(8,128)} %copy-done.111) | copy-start | bytes 98308
  130.7 115.5 %copy-start.119 = (f32[5,8,8,128]{3,1,2,0:T(8,128)S(1)}, f32[5,8,8,128]{3,1,2,0:T(8,128)}, u32[]{:S(2)}) copy-start(f32[5,8,8,128]{3,1,2,0:T(8,128)} %copy-done.118) | copy-start | bytes 491524
  247.1 19.8 %copy-start.166 = (pred[128]{0:T(512)(128)(4,1)S(1)}, pred[128]{0:T(512)(128)(4,1)}, u32[]{:S(2)}) copy-start(pred[128]{0:T(512)(128)(4,1)} %eq.100) | copy-start | bytes 388
  247.1 19.8 %copy-start.167 = (pred[128]{0:T(512)(128)(4,1)S(1)}, pred[128]{0:T(512)(128)(4,1)}, u32[]{:S(2)}) copy-start(pred[128]{0:T(512)(128)(4,1)} %eq.98) | copy-start | bytes 388
  247.1 19.8 %copy-start.168 = (pred[128]{0:T(512)(128)(4,1)S(1)}, pred[128]{0:T(512)(128)(4,1)}, u32[]{:S(2)}) copy-start(pred[128]{0:T(512)(128)(4,1)} %eq.91) | copy-start | bytes 388
  247.1 19.8 %copy-start.169 = (pred[128]{0:T(512)(128)(4,1)S(1)}, pred[128]{0:T(512)(128)(4,1)}, u32[]{:S(2)}) copy-start(pred[128]{0:T(512)(128)(4,1)} %lt.72) | copy-start | bytes 388
  247.9 19.2 %copy-start.48 = (f32[5,8,1,8,128]{4,2,0,1,3:T(1,128)S(1)}, f32[5,8,1,8,128]{4,2,0,1,3:T(1,128)}, u32[]{:S(2)}) copy-start(f32[5,8,1,8,128]{4,2,0,1,3:T(1,128)} %get-tuple-element.100) | copy-start | bytes 491524
  247.9 19.2 %copy-start.153 = (s32[128]{0:T(128)S(1)}, s32[128]{0:T(128)}, u32[]{:S(2)}) copy-start(s32[128]{0:T(128)} %copy-done.151) | copy-start | bytes 1540
  248.8 21.5 %copy-start.135 = (f32[8,8,1,1]{1,0,3,2:T(8,128)S(1)}, f32[8,8,1,1]{1,0,3,2:T(8,128)}, u32[]{:S(2)}) copy-start(f32[8,8,1,1]{1,0,3,2:T(8,128)} %constant.274) | copy-start | bytes 772
  248.8 19.5 %collective-permute-start.7 = (f32[5,8,8,32]{3,1,2,0:T(8,128)S(1)}, f32[5,8,8,32]{3,1,2,0:T(8,128)S(1)}, u32[]{:S(2)}, u32[]{:S(2)}) collective-permute-start(f32[5,8,8,32]{3,1,2,0:T(8,128)S(1)} %get-tuple-element.202), channel_id=1, source_target_pairs={{752,0},{760,8},{0,16},{8,24},{16,32},{24,40},{32,48},{40,56},{48,... | collective-permute-start | bytes 122888 | tf_op jit(solution)/shard_map/ppermute | solution.py:20
  250.7 19.3 %collective-permute-start.6 = (f32[5,8,8,32]{3,1,2,0:T(8,128)S(1)}, f32[5,8,8,32]{3,1,2,0:T(8,128)S(1)}, u32[]{:S(2)}, u32[]{:S(2)}) collective-permute-start(f32[5,8,8,32]{3,1,2,0:T(8,128)S(1)} %get-tuple-element.203), channel_id=1, source_target_pairs={{16,0},{24,8},{32,16},{40,24},{48,32},{56,40},{64,48},{72,56},{80,... | collective-permute-start | bytes 122888 | tf_op jit(solution)/shard_map/ppermute | solution.py:20
  258.3 11.7 %collective-permute-start.5 = (f32[5,8,8,32]{3,1,2,0:T(8,128)S(1)}, f32[5,8,8,32]{3,1,2,0:T(8,128)S(1)}, u32[]{:S(2)}, u32[]{:S(2)}) collective-permute-start(f32[5,8,8,32]{3,1,2,0:T(8,128)S(1)} %get-tuple-element.204), channel_id=1, source_target_pairs={{760,0},{0,8},{8,16},{16,24},{24,32},{32,40},{40,48},{48,56},{56,6... | collective-permute-start | bytes 122888 | tf_op jit(solution)/shard_map/ppermute | solution.py:20
  260.2 9.8 %collective-permute-start.4 = (f32[5,8,8,32]{3,1,2,0:T(8,128)S(1)}, f32[5,8,8,32]{3,1,2,0:T(8,128)S(1)}, u32[]{:S(2)}, u32[]{:S(2)}) collective-permute-start(f32[5,8,8,32]{3,1,2,0:T(8,128)S(1)} %get-tuple-element.201), channel_id=1, source_target_pairs={{8,0},{16,8},{24,16},{32,24},{40,32},{48,40},{56,48},{64,56},{72,6... | collective-permute-start | bytes 122888 | tf_op jit(solution)/shard_map/ppermute | solution.py:20
  268.2 16.9 %collective-permute-start.9 = (f32[1,5,8,8,128]{4,3,1,2,0:T(8,128)}, f32[1,5,8,8,128]{4,3,1,2,0:T(8,128)S(1)}, u32[]{:S(2)}, u32[]{:S(2)}) collective-permute-start(f32[1,5,8,8,128]{4,3,1,2,0:T(8,128)} %bitcast.1337), channel_id=1, source_target_pairs={{1,0},{2,1},{3,2},{4,3},{5,4},{6,5},{7,6},{0,7},{9,8},{10,9},{11,1... | collective-permute-start | bytes 491528 | tf_op jit(solution)/shard_map/ppermute | solution.py:32
  350.6 22.2 %copy-start.173 = (pred[128]{0:T(512)(128)(4,1)S(1)}, pred[128]{0:T(512)(128)(4,1)}, u32[]{:S(2)}) copy-start(pred[128]{0:T(512)(128)(4,1)} %copy-done.172) | copy-start | bytes 388
  350.6 22.1 %copy-start.115 = (f32[5,8,8,1,128]{4,1,0,2,3:T(8,128)}, f32[5,8,8,1,128]{4,1,0,2,3:T(8,128)S(1)}, u32[]{:S(2)}) copy-start(f32[5,8,8,1,128]{4,1,0,2,3:T(8,128)S(1)} %constant_dynamic-update-slice_fusion.122) | copy-start | bytes 491524
  351.3 81.1 %collective-permute-start.19 = (f32[1,5,8,8,128]{4,2,3,1,0:T(8,128)}, f32[1,5,8,8,128]{4,2,3,1,0:T(8,128)S(1)}, u32[]{:S(2)}, u32[]{:S(2)}) collective-permute-start(f32[1,5,8,8,128]{4,2,3,1,0:T(8,128)} %get-tuple-element.79), channel_id=1, source_target_pairs={{1,0},{2,1},{3,2},{4,3},{5,4},{6,5},{7,6},{0,7},{9,8},{10,9},{11,1... | collective-permute-start | bytes 491528 | tf_op jit(solution)/shard_map/ppermute | solution.py:32
  353.9 52.5 %collective-permute-start.13 = (f32[5,8,8,32]{3,1,2,0:T(8,128)}, f32[5,8,8,32]{3,1,2,0:T(8,128)}, u32[]{:S(2)}, u32[]{:S(2)}) collective-permute-start(f32[5,8,8,32]{3,1,2,0:T(8,128)} %get-tuple-element.194), channel_id=1, source_target_pairs={{16,0},{24,8},{32,16},{40,24},{48,32},{56,40},{64,48},{72,56},{80,... | collective-permute-start | bytes 122888 | tf_op jit(solution)/shard_map/ppermute | solution.py:20
  357.5 48.9 %collective-permute-start.12 = (f32[5,8,8,32]{3,1,2,0:T(8,128)}, f32[5,8,8,32]{3,1,2,0:T(8,128)}, u32[]{:S(2)}, u32[]{:S(2)}) collective-permute-start(f32[5,8,8,32]{3,1,2,0:T(8,128)} %get-tuple-element.195), channel_id=1, source_target_pairs={{752,0},{760,8},{0,16},{8,24},{16,32},{24,40},{32,48},{40,56},{48,... | collective-permute-start | bytes 122888 | tf_op jit(solution)/shard_map/ppermute | solution.py:20
  360.1 46.3 %collective-permute-start.11 = (f32[5,8,8,32]{3,1,2,0:T(8,128)}, f32[5,8,8,32]{3,1,2,0:T(8,128)}, u32[]{:S(2)}, u32[]{:S(2)}) collective-permute-start(f32[5,8,8,32]{3,1,2,0:T(8,128)} %get-tuple-element.196), channel_id=1, source_target_pairs={{8,0},{16,8},{24,16},{32,24},{40,32},{48,40},{56,48},{64,56},{72,6... | collective-permute-start | bytes 122888 | tf_op jit(solution)/shard_map/ppermute | solution.py:20
  370.8 35.6 %collective-permute-start.10 = (f32[5,8,8,32]{3,1,2,0:T(8,128)}, f32[5,8,8,32]{3,1,2,0:T(8,128)}, u32[]{:S(2)}, u32[]{:S(2)}) collective-permute-start(f32[5,8,8,32]{3,1,2,0:T(8,128)} %get-tuple-element.193), channel_id=1, source_target_pairs={{760,0},{0,8},{8,16},{16,24},{24,32},{32,40},{40,48},{48,56},{56,6... | collective-permute-start | bytes 122888 | tf_op jit(solution)/shard_map/ppermute | solution.py:20
  408.0 20.1 %copy-start.154 = (s32[128]{0:T(128)S(1)}, s32[128]{0:T(128)}, u32[]{:S(2)}) copy-start(s32[128]{0:T(128)} %copy-done.151) | copy-start | bytes 1540
  408.7 20.3 %copy-start.30 = (f32[5,8,1,8,128]{4,2,0,1,3:T(1,128)S(1)}, f32[5,8,1,8,128]{4,2,0,1,3:T(1,128)}, u32[]{:S(2)}) copy-start(f32[5,8,1,8,128]{4,2,0,1,3:T(1,128)} %get-tuple-element.63) | copy-start | bytes 491524
  408.7 20.3 %copy-start.31 = (f32[5,8,1,8,128]{4,2,0,1,3:T(1,128)S(1)}, f32[5,8,1,8,128]{4,2,0,1,3:T(1,128)}, u32[]{:S(2)}) copy-start(f32[5,8,1,8,128]{4,2,0,1,3:T(1,128)} %get-tuple-element.64) | copy-start | bytes 491524
  408.7 20.3 %copy-start.32 = (f32[5,8,1,8,128]{4,2,0,1,3:T(1,128)S(1)}, f32[5,8,1,8,128]{4,2,0,1,3:T(1,128)}, u32[]{:S(2)}) copy-start(f32[5,8,1,8,128]{4,2,0,1,3:T(1,128)} %get-tuple-element.65) | copy-start | bytes 491524
  408.7 20.3 %copy-start.33 = (f32[5,8,1,8,128]{4,2,0,1,3:T(1,128)S(1)}, f32[5,8,1,8,128]{4,2,0,1,3:T(1,128)}, u32[]{:S(2)}) copy-start(f32[5,8,1,8,128]{4,2,0,1,3:T(1,128)} %get-tuple-element.68) | copy-start | bytes 491524
  408.7 20.3 %copy-start.34 = (f32[5,8,1,8,128]{4,2,0,1,3:T(1,128)S(1)}, f32[5,8,1,8,128]{4,2,0,1,3:T(1,128)}, u32[]{:S(2)}) copy-start(f32[5,8,1,8,128]{4,2,0,1,3:T(1,128)} %get-tuple-element.69) | copy-start | bytes 491524
  408.7 20.3 %copy-start.35 = (f32[5,8,1,8,128]{4,2,0,1,3:T(1,128)S(1)}, f32[5,8,1,8,128]{4,2,0,1,3:T(1,128)}, u32[]{:S(2)}) copy-start(f32[5,8,1,8,128]{4,2,0,1,3:T(1,128)} %get-tuple-element.70) | copy-start | bytes 491524
  409.4 18.6 %copy-start.73 = (f32[5,8,8,128]{3,2,1,0:T(8,128)S(1)}, f32[5,8,8,128]{3,2,1,0:T(8,128)}, u32[]{:S(2)}) copy-start(f32[5,8,8,128]{3,2,1,0:T(8,128)} %reverse_bitcast_fusion) | copy-start | bytes 491524
  409.4 18.6 %copy-start.74 = (f32[5,8,8,128]{3,2,1,0:T(8,128)S(1)}, f32[5,8,8,128]{3,2,1,0:T(8,128)}, u32[]{:S(2)}) copy-start(f32[5,8,8,128]{3,2,1,0:T(8,128)} %rev.55) | copy-start | bytes 491524
  409.6 20.7 %copy-start.38 = (f32[5,8,1,8,128]{4,2,0,1,3:T(1,128)S(1)}, f32[5,8,1,8,128]{4,2,0,1,3:T(1,128)}, u32[]{:S(2)}) copy-start(f32[5,8,1,8,128]{4,2,0,1,3:T(1,128)} %get-tuple-element.62) | copy-start | bytes 491524
  409.6 21.1 %collective-permute-start.17 = (f32[5,8,8,32]{3,1,2,0:T(8,128)S(1)}, f32[5,8,8,32]{3,1,2,0:T(8,128)S(1)}, u32[]{:S(2)}, u32[]{:S(2)}) collective-permute-start(f32[5,8,8,32]{3,1,2,0:T(8,128)S(1)} %get-tuple-element.188), channel_id=1, source_target_pairs={{752,0},{760,8},{0,16},{8,24},{16,32},{24,40},{32,48},{40,56},{48,... | collective-permute-start | bytes 122888 | tf_op jit(solution)/shard_map/ppermute | solution.py:20
  411.7 19.0 %collective-permute-start.16 = (f32[5,8,8,32]{3,1,2,0:T(8,128)S(1)}, f32[5,8,8,32]{3,1,2,0:T(8,128)S(1)}, u32[]{:S(2)}, u32[]{:S(2)}) collective-permute-start(f32[5,8,8,32]{3,1,2,0:T(8,128)S(1)} %get-tuple-element.189), channel_id=1, source_target_pairs={{16,0},{24,8},{32,16},{40,24},{48,32},{56,40},{64,48},{72,56},{80,... | collective-permute-start | bytes 122888 | tf_op jit(solution)/shard_map/ppermute | solution.py:20
  419.3 11.4 %collective-permute-start.15 = (f32[5,8,8,32]{3,1,2,0:T(8,128)S(1)}, f32[5,8,8,32]{3,1,2,0:T(8,128)S(1)}, u32[]{:S(2)}, u32[]{:S(2)}) collective-permute-start(f32[5,8,8,32]{3,1,2,0:T(8,128)S(1)} %get-tuple-element.190), channel_id=1, source_target_pairs={{760,0},{0,8},{8,16},{16,24},{24,32},{32,40},{40,48},{48,56},{56,6... | collective-permute-start | bytes 122888 | tf_op jit(solution)/shard_map/ppermute | solution.py:20
  421.5 9.2 %collective-permute-start.14 = (f32[5,8,8,32]{3,1,2,0:T(8,128)S(1)}, f32[5,8,8,32]{3,1,2,0:T(8,128)S(1)}, u32[]{:S(2)}, u32[]{:S(2)}) collective-permute-start(f32[5,8,8,32]{3,1,2,0:T(8,128)S(1)} %get-tuple-element.187), channel_id=1, source_target_pairs={{8,0},{16,8},{24,16},{32,24},{40,32},{48,40},{56,48},{64,56},{72,6... | collective-permute-start | bytes 122888 | tf_op jit(solution)/shard_map/ppermute | solution.py:20
  434.9 5.5 %collective-permute-start.18 = (f32[1,5,8,8,128]{4,2,1,3,0:T(8,128)S(1)}, f32[1,5,8,8,128]{4,2,1,3,0:T(8,128)S(1)}, u32[]{:S(2)}, u32[]{:S(2)}) collective-permute-start(f32[1,5,8,8,128]{4,2,1,3,0:T(8,128)S(1)} %bitcast.1395), channel_id=1, source_target_pairs={{0,1},{1,2},{2,3},{3,4},{4,5},{5,6},{6,7},{7,0},{8,9},{9,10},{10,1... | collective-permute-start | bytes 491528 | tf_op jit(solution)/shard_map/ppermute | solution.py:29
  (160 other events, 543.3 us)
where the time goes:
time: 456 us; the launch traced here: 450 us
  local copies, waits for them, and re-layouts  132 us (29%)
  blocking collectives  108 us (24%)
  other arithmetic  103 us (23%)
  starting transfers between devices  93.2 us (20%)
  matrix products  6.86 us (2%)
  between operations  4.9 us (1%)
    pmax x1, blocking collectives, on_device(): fastest = lax.pmax(jnp.max(wave_speed(state5, metric)), ('slab', 'cut'))  108 us
    ppermute x16, starting transfers between devices, passed_along(): return lax.ppermute(block, axis, route)  84.1 us
    add x18, other arithmetic, derive_lifted(): total + float(differ_table[target, source]) * lax.index_in_dim(flux, sour...  42.5 us
    gather x8, local copies, waits for them, and re-layouts, take_last(): return jnp.take_along_axis(values, shaped, axis=-1)  28 us
    unnamed x422, local copies, waits for them, and re-layouts  20.9 us
    gather x4, local copies, waits for them, and re-layouts, mortar_terms(): fine_trace = jnp.take(current[:, :, 0], fine_index, axis=3)  13.5 us
    unnamed x64, other arithmetic  13 us
    another operation x6, local copies, waits for them, and re-layouts, derive_lifted(): return jnp.stack(rows, axis=axis)  10.2 us
  transfers between devices with their start and end apart: 20, of which 1 were waited for; matrix products, arithmetic and copies ran while one was open for 35% of the time, Pallas kernels for 0%

commit v1 on v0

v1 whole, which is shorter than its diff:
```python
import functools

import jax
import jax.numpy as jnp
import numpy as np
from jax import lax
from jax.experimental import pallas as pl
from jax.experimental.pallas import tpu as pltpu
from jax.sharding import PartitionSpec as P

NP = 8
NVAR = 5
FACE = NP * NP
LANES = 128
OFFS = 4
CAP = 32
MESH = pl.DeviceIdType.MESH

section_a = (0.0, -567301805773.0 / 1357537059087.0)
section_b = (1432997174477.0 / 9575080441755.0, 5161836677717.0 / 13612068292357.0)


def legendre_rows(points, node_count):
    legendre = np.zeros((node_count, node_count))
    legendre[:, 0] = 1.0
    legendre[:, 1] = points
    for degree in range(2, node_count):
        legendre[:, degree] = (
            (2 * degree - 1) * points * legendre[:, degree - 1]
            - (degree - 1) * legendre[:, degree - 2]
        ) / degree
    return legendre


def lobatto(node_count):
    poly_order = node_count - 1
    points = -np.cos(np.pi * np.arange(node_count) / poly_order)
    for newton_step in range(40):
        legendre = legendre_rows(points, node_count)
        points = points - (points * legendre[:, poly_order] - legendre[:, poly_order - 1]) / (
            node_count * legendre[:, poly_order]
        )
    top_row = legendre_rows(points, node_count)[:, poly_order]
    weights = 2.0 / (poly_order * node_count * top_row * top_row)
    differ = np.zeros((node_count, node_count))
    for target in range(node_count):
        for source in range(node_count):
            if target != source:
                differ[target, source] = top_row[target] / (
                    top_row[source] * (points[target] - points[source])
                )
    differ[0, 0] = -poly_order * node_count / 4.0
    differ[poly_order, poly_order] = poly_order * node_count / 4.0
    lower_half = np.zeros((node_count, node_count))
    targets = (points - 1) / 2.0
    for source in range(node_count):
        basis = np.ones(node_count)
        for other in range(node_count):
            if other != source:
                basis = basis * (targets - points[other]) / (points[source] - points[other])
        lower_half[:, source] = basis
    lower_back = 0.5 * np.transpose(lower_half) * weights[None, :] / weights[:, None]
    return (weights, differ, lower_half, lower_back)


WEIGHTS, DIFFER, HALF, BACK = lobatto(NP)
LIFT = float(1.0 / WEIGHTS[0])
EVEN = 0.5 * (DIFFER[:4, :4] + DIFFER[:4, :3:-1])
ODD = 0.5 * (DIFFER[:4, :4] - DIFFER[:4, :3:-1])


def combine(row, values):
    total = None
    for weight, value in zip(row, values):
        weight = float(np.float32(weight))
        if abs(weight) < 1e-12:
            continue
        term = value if weight == 1.0 else weight * value
        total = term if total is None else total + term
    return total


def derive(f):
    even = [f[j] + f[7 - j] for j in range(4)]
    odd = [f[j] - f[7 - j] for j in range(4)]
    out = [None] * 8
    for i in range(4):
        from_even = combine(EVEN[i], even)
        from_odd = combine(ODD[i], odd)
        out[i] = from_odd + from_even
        out[7 - i] = from_odd - from_even
    return out


def half_map(matrix, upper, f):
    f = [jnp.where(upper, f[7 - j], f[j]) for j in range(8)]
    g = [combine(matrix[i], f) for i in range(8)]
    return [jnp.where(upper, g[7 - i], g[i]) for i in range(8)]


def primitives(u):
    inverse = 1.0 / u[0]
    velocity = [u[1] * inverse, u[2] * inverse, u[3] * inverse]
    carried = u[1] * velocity[0] + u[2] * velocity[1] + u[3] * velocity[2]
    pressure = 0.4 * (u[4] - 0.5 * carried)
    return inverse, velocity, pressure


def flux_of(u, normal, pressure, direction):
    rows = [u[1 + direction]]
    for column in range(3):
        carried = u[1 + column] * normal
        rows.append(carried + pressure if column == direction else carried)
    rows.append(normal * (u[4] + pressure))
    return rows


def face_flux(u, direction):
    inverse, velocity, pressure = primitives(u)
    normal = velocity[direction]
    speed = jnp.abs(normal) + jnp.sqrt(1.4 * pressure * inverse)
    return flux_of(u, normal, pressure, direction), speed


def face_parts(left, right, direction):
    left_flux, left_speed = face_flux(left, direction)
    right_flux, right_speed = face_flux(right, direction)
    half_speed = 0.5 * jnp.maximum(left_speed, right_speed)
    mean = [0.5 * (r - l) for l, r in zip(left_flux, right_flux)]
    jump = [half_speed * (r - l) for l, r in zip(left, right)]
    return mean, jump


def lane_pick(x, index):
    return jnp.take_along_axis(x, index, axis=1, mode="promise_in_bounds")


def swap_blocks(x, lane):
    high = lane >= 64
    odd = (lane // 32) % 2 == 1
    y = list(x)
    for k in (0, 1):
        y[k] = jnp.where(high, pltpu.roll(x[k + 2], 64, 1), x[k])
        y[k + 2] = jnp.where(high, x[k + 2], pltpu.roll(x[k], 64, 1))
    z = list(y)
    for k in (0, 2):
        z[k] = jnp.where(odd, pltpu.roll(y[k + 1], 32, 1), y[k])
        z[k + 1] = jnp.where(odd, y[k + 1], pltpu.roll(y[k], 96, 1))
    return z


def offset_distance(offset_index):
    return (offset_index // 2 + 1) * (1 - 2 * (offset_index % 2))


def eight(row):
    return jnp.broadcast_to(row, (8, LANES))


def tile(i):
    return pl.ds(pl.multiple_of(i * 8, 8), 8)


def kernel(
    slabs, cuts, ys, zs,
    u_ref, ints_ref,
    adv_ref, reg_ref,
    prim, rate, sect,
    zsend, zrecv, csend, crecv, fsend, frecv,
    vsend, vrecv,
    own_coarse, own_fine, far_coarse, far_fine, work, packed,
    zs_sem, zr_sem, cs_sem, cr_sem, fs_sem, fr_sem, vs_sem, vr_sem,
):
    s = lax.axis_index("slab")
    t = lax.axis_index("cut")
    y = s // zs
    z = s % zs
    cut_peers = [(s, (t + d) % cuts) for d in range(1, cuts)]
    y_peers = [(((y + d) % ys) * zs + z, t) for d in range(1, ys)]
    z_peers = [(y * zs + (z + d) % zs, t) for d in range(1, zs)]
    ahead = [((s + offset_distance(o) + slabs) % slabs, t) for o in range(OFFS)]
    back = [((s - offset_distance(o) + slabs) % slabs, t) for o in range(OFFS)]

    barrier = pltpu.get_barrier_semaphore()
    greeted = cut_peers + y_peers + z_peers + ahead
    for peer in greeted:
        pl.semaphore_signal(barrier, inc=1, device_id=peer, device_id_type=MESH)

    lane = lax.broadcasted_iota(jnp.int32, (8, LANES), 1)
    sub = lax.broadcasted_iota(jnp.int32, (8, LANES), 0)
    flipped = 7 - sub
    spread = lax.broadcasted_iota(jnp.int32, (LANES, LANES), 0)
    counting = (lane + 1).astype(jnp.float32)

    level = eight(ints_ref[0:1])
    neighbour = eight(ints_ref[1:2])
    coarse_index = eight(ints_ref[2:3])
    quadrant = eight(ints_ref[3:4])
    fine_index = eight(ints_ref[4:5])
    turns = eight(ints_ref[5:6])
    coarse_live = eight(ints_ref[6:7]) > 0
    fine_live = eight(ints_ref[7:8]) > 0
    metric = jnp.where(level == 0, 1.0, jnp.where(level == 1, 2.0, 4.0))
    own_a = quadrant >= 2
    own_c = quadrant % 2 == 1
    back_turns = (4 - turns) % 4

    def inverse_of(row, counts):
        table = jnp.where(spread == row, 1.0, 0.0).astype(jnp.bfloat16)
        found = lax.dot_general(
            counts.astype(jnp.bfloat16), table, (((1,), (1,)), ((), ())),
            preferred_element_type=jnp.float32,
        )
        present = found > 0.5
        return jnp.maximum(found - 1.0, 0.0).astype(jnp.int32), present

    x_source, _ = inverse_of(ints_ref[1:2], counting)
    c_source, c_present = inverse_of(
        ints_ref[2:3], jnp.where(lane % 4 == 0, counting, 0.0)
    )
    f_source, f_present = inverse_of(ints_ref[4:5], counting)
    group_pick = (lane // 32) * 32 + (lane % 8) * 4
    group_index = lane_pick(coarse_index, group_pick)
    group_block = (lane // 8) % 4
    widen = [(lane // 32) * 32 + k * 8 + (lane % 32) // 4 for k in range(4)]

    def rev(x):
        return jnp.take_along_axis(x, flipped, axis=0, mode="promise_in_bounds")

    def rotated(ref, v, amount):
        odd = amount % 2 == 1
        far = amount >= 2
        mixed = [
            jnp.where(odd, ref[v, pl.ds(7 - i, 8, stride=8), :], ref[v, pl.ds(8 * i, 8), :])
            for i in range(8)
        ]
        return [jnp.where(far, rev(mixed[7 - i]), mixed[i]) for i in range(8)]

    def half_both(matrix, upper_a, upper_c, values, v):
        along_a = half_map(matrix, upper_a, values)
        for i in range(8):
            work[v, pl.ds(8 * i, 8), :] = along_a[i]
        columns = [work[v, pl.ds(j, 8, stride=8), :] for j in range(8)]
        return half_map(matrix, upper_c, columns)

    def send_mortars(state, stage):
        def one(v, carry):
            top = [state[v, pl.ds(64 * a + 56, 8), :] for a in range(8)]
            for h in range(2):
                pack = lane_pick(top[4 * h], group_index)
                for k in range(1, 4):
                    pack = jnp.where(group_block == k, lane_pick(top[4 * h + k], group_index), pack)
                packed[2 * v + h] = pack
            for a in range(8):
                work[v, pl.ds(8 * a, 8), :] = lane_pick(state[v, pl.ds(64 * a, 8), :], fine_index)
            turned = rotated(work, v, back_turns)
            for a in range(8):
                own_fine[v, pl.ds(8 * a, 8), :] = turned[a]
            for h in range(2):
                blocks = swap_blocks(turned[4 * h : 4 * h + 4], lane)
                for o in range(OFFS):
                    fsend[stage, o, tile(2 * v + h), :] = blocks[o]
            return carry

        lax.fori_loop(0, NVAR, one, 0)
        packed[10] = quadrant.astype(jnp.float32)
        packed[11] = jnp.zeros((8, LANES), jnp.float32)
        for m in range(3):
            blocks = swap_blocks([packed[4 * m + k] for k in range(4)], lane)
            for o in range(OFFS):
                csend[stage, o, pl.ds(8 * m, 8), :] = blocks[o]

    def mortar_copies(stage):
        copies = []
        for o in range(OFFS):
            copies.append(pltpu.make_async_remote_copy(
                src_ref=fsend.at[stage, o], dst_ref=frecv.at[stage, o],
                send_sem=fs_sem.at[stage, o], recv_sem=fr_sem.at[stage, o],
                device_id=back[o], device_id_type=MESH))
            copies.append(pltpu.make_async_remote_copy(
                src_ref=csend.at[stage, o], dst_ref=crecv.at[stage, o],
                send_sem=cs_sem.at[stage, o], recv_sem=cr_sem.at[stage, o],
                device_id=ahead[o], device_id_type=MESH))
        return copies

    def z_copies(stage):
        targets = [(s, (t + 1) % cuts), (s, (t + cuts - 1) % cuts)]
        return [
            pltpu.make_async_remote_copy(
                src_ref=zsend.at[stage, i], dst_ref=zrecv.at[stage, i],
                send_sem=zs_sem.at[stage, i], recv_sem=zr_sem.at[stage, i],
                device_id=targets[i], device_id_type=MESH)
            for i in range(2)
        ]

    def z_traces(state, stage):
        for v in range(NVAR):
            zsend[stage, 0, v] = state[v, pl.ds(7, FACE, stride=8), :]
            zsend[stage, 1, v] = state[v, pl.ds(0, FACE, stride=8), :]

    def own_interpolated(state):
        def one(v, carry):
            picked = [lane_pick(state[v, pl.ds(64 * a + 56, 8), :], coarse_index) for a in range(8)]
            columns = half_both(HALF, own_a, own_c, picked, v)
            for j in range(8):
                own_coarse[v, pl.ds(j, 8, stride=8), :] = columns[j]
            return carry

        lax.fori_loop(0, NVAR, one, 0)

    def primitive_pass(state, with_speed):
        def one(i, fastest):
            rows = pl.ds(pl.multiple_of(i * 32, 32), 32)
            u = [state[v, rows, :] for v in range(NVAR)]
            inverse, velocity, pressure = primitives(u)
            for d in range(3):
                prim[d, rows, :] = velocity[d]
            prim[3, rows, :] = pressure
            if not with_speed:
                return fastest
            square = velocity[0] * velocity[0] + velocity[1] * velocity[1] + velocity[2] * velocity[2]
            speed = jnp.sqrt(square) + jnp.sqrt(1.4 * pressure * inverse)
            return jnp.maximum(fastest, speed)

        start = jnp.zeros((32, LANES) if with_speed else (8, LANES), jnp.float32)
        return lax.fori_loop(0, 16, one, start)

    def volume(state):
        def line(read, normal, pressure, direction, v):
            if v == 0:
                return [read(1 + direction, j) for j in range(8)]
            if v == 4:
                return [normal[j] * (read(4, j) + pressure[j]) for j in range(8)]
            if v == 1 + direction:
                return [read(v, j) * normal[j] + pressure[j] for j in range(8)]
            return [read(v, j) * normal[j] for j in range(8)]

        def z_pass(a, carry):
            def at(j):
                return pl.ds(a * 64 + j, 8, stride=8)

            normal = [prim[2, at(j), :] for j in range(8)]
            pressure = [prim[3, at(j), :] for j in range(8)]
            for v in range(NVAR):
                out = derive(line(lambda w, j: state[w, at(j), :], normal, pressure, 2, v))
                for j in range(8):
                    rate[v, at(j), :] = out[j]
            return carry

        def y_pass(a, carry):
            def at(j):
                return pl.ds(pl.multiple_of(a * 64 + j * 8, 8), 8)

            normal = [prim[1, at(j), :] for j in range(8)]
            pressure = [prim[3, at(j), :] for j in range(8)]
            for v in range(NVAR):
                out = derive(line(lambda w, j: state[w, at(j), :], normal, pressure, 1, v))
                for j in range(8):
                    rate[v, at(j), :] += out[j]
            return carry

        def x_pass(b, carry):
            def at(j):
                return pl.ds(pl.multiple_of(b * 8 + j * 64, 8), 8)

            normal = [prim[0, at(j), :] for j in range(8)]
            pressure = [prim[3, at(j), :] for j in range(8)]
            for v in range(NVAR):
                out = derive(line(lambda w, j: state[w, at(j), :], normal, pressure, 0, v))
                for j in range(8):
                    rate[v, at(j), :] += out[j]
            return carry

        lax.fori_loop(0, 8, z_pass, 0)
        lax.fori_loop(0, 8, y_pass, 0)
        lax.fori_loop(0, 8, x_pass, 0)

    def x_faces(state):
        def one(i, carry):
            low = pl.ds(pl.multiple_of(i * 16, 16), 16)
            high = pl.ds(pl.multiple_of(448 + i * 16, 16), 16)
            pick = jnp.broadcast_to(ints_ref[1:2], (16, LANES))
            source = jnp.concatenate([x_source, x_source], axis=0)
            left = [state[v, high, :] for v in range(NVAR)]
            right = [lane_pick(state[v, low, :], pick) for v in range(NVAR)]
            mean, jump = face_parts(left, right, 0)
            for v in range(NVAR):
                rate[v, high, :] += LIFT * (mean[v] - jump[v])
                rate[v, low, :] += LIFT * lane_pick(mean[v] + jump[v], source)
            return carry

        lax.fori_loop(0, 4, one, 0)

    def z_faces(stage):
        def one(i, carry):
            rows = pl.ds(pl.multiple_of(i * 16, 16), 16)
            bottom = pl.ds(i * 128, 16, stride=8)
            top = pl.ds(i * 128 + 7, 16, stride=8)
            left = [zsend[stage, 0, v, rows, :] for v in range(NVAR)]
            right = [zrecv[stage, 1, v, rows, :] for v in range(NVAR)]
            mean, jump = face_parts(left, right, 2)
            for v in range(NVAR):
                rate[v, top, :] += LIFT * (mean[v] - jump[v])
            left = [zrecv[stage, 0, v, rows, :] for v in range(NVAR)]
            right = [zsend[stage, 1, v, rows, :] for v in range(NVAR)]
            mean, jump = face_parts(left, right, 2)
            for v in range(NVAR):
                rate[v, bottom, :] += LIFT * (mean[v] + jump[v])
            return carry

        lax.fori_loop(0, 4, one, 0)

    def mortars(stage):
        for m in range(3):
            blocks = swap_blocks([crecv[stage, o, pl.ds(8 * m, 8), :] for o in range(OFFS)], lane)
            for k in range(4):
                packed[4 * m + k] = blocks[k]
        far_quadrant = packed[10]
        far_a = far_quadrant > 1.5
        far_c = (far_quadrant == 1.0) | (far_quadrant == 3.0)

        def expand(v, carry):
            for h in range(2):
                blocks = swap_blocks([frecv[stage, o, tile(2 * v + h), :] for o in range(OFFS)], lane)
                for k in range(4):
                    far_fine[v, pl.ds(8 * (4 * h + k), 8), :] = blocks[k]
            picked = [lane_pick(packed[2 * v + a // 4], widen[a % 4]) for a in range(8)]
            columns = half_both(HALF, far_a, far_c, picked, v)
            for j in range(8):
                far_coarse[v, pl.ds(j, 8, stride=8), :] = columns[j]
            return carry

        lax.fori_loop(0, NVAR, expand, 0)

        def fluxes(i, carry):
            rows = pl.ds(pl.multiple_of(i * 16, 16), 16)
            live = jnp.concatenate([coarse_live, coarse_live], axis=0)
            left = [own_coarse[v, rows, :] for v in range(NVAR)]
            right = [far_fine[v, rows, :] for v in range(NVAR)]
            mean, jump = face_parts(left, right, 1)
            for v in range(NVAR):
                own_coarse[v, rows, :] = jnp.where(live, mean[v] - jump[v], 0.0)
            live = jnp.concatenate([fine_live, fine_live], axis=0)
            left = [far_coarse[v, rows, :] for v in range(NVAR)]
            right = [own_fine[v, rows, :] for v in range(NVAR)]
            mean, jump = face_parts(left, right, 1)
            for v in range(NVAR):
                own_fine[v, rows, :] = jnp.where(live, mean[v] + jump[v], 0.0)
            return carry

        lax.fori_loop(0, 4, fluxes, 0)

        def scatter(v, carry):
            values = [own_coarse[v, pl.ds(8 * a, 8), :] for a in range(8)]
            columns = half_both(BACK, own_a, own_c, values, v)
            for c in range(8):
                total = columns[c] + pltpu.roll(columns[c], 127, 1)
                total = total + pltpu.roll(total, 126, 1)
                share = jnp.where(c_present, lane_pick(total, c_source), 0.0)
                rate[v, pl.ds(56 + c, 8, stride=64), :] += LIFT * share
            turned = rotated(own_fine, v, turns)
            for a in range(8):
                share = jnp.where(f_present, lane_pick(turned[a], f_source), 0.0)
                rate[v, pl.ds(64 * a, 8), :] += LIFT * share
            return carry

        lax.fori_loop(0, NVAR, scatter, 0)

    def speed_round(first, peers):
        return [
            pltpu.make_async_remote_copy(
                src_ref=vsend.at[0 if first == 0 else (1 if first == cuts - 1 else 2)],
                dst_ref=vrecv.at[first + i],
                send_sem=vs_sem.at[first + i], recv_sem=vr_sem.at[first + i],
                device_id=peer, device_id_type=MESH)
            for i, peer in enumerate(peers)
        ]

    def finish_round(copies, value, first):
        for copy in copies:
            copy.wait_recv()
        for i in range(len(copies)):
            value = jnp.maximum(value, vrecv[first + i])
        return value

    speed = primitive_pass(u_ref, True)
    speed = jnp.maximum(jnp.maximum(speed[0:8], speed[8:16]), jnp.maximum(speed[16:24], speed[24:32]))
    speed = speed * metric
    vsend[0] = speed
    pl.semaphore_wait(barrier, len(greeted))
    round_1 = speed_round(0, cut_peers)
    for copy in round_1:
        copy.start()
    started = list(round_1)
    z_traces(u_ref, 0)
    zc = z_copies(0)
    for copy in zc:
        copy.start()
    send_mortars(u_ref, 0)
    mc = mortar_copies(0)
    for copy in mc:
        copy.start()
    started += zc + mc
    own_interpolated(u_ref)
    speed = finish_round(round_1, speed, 0)
    vsend[1] = speed
    round_2 = speed_round(cuts - 1, y_peers)
    for copy in round_2:
        copy.start()
    started += round_2
    volume(u_ref)
    speed = finish_round(round_2, speed, cuts - 1)
    vsend[2] = speed
    round_3 = speed_round(cuts + ys - 2, z_peers)
    for copy in round_3:
        copy.start()
    started += round_3
    x_faces(u_ref)
    for copy in zc:
        copy.wait_recv()
    z_faces(0)
    for copy in mc:
        copy.wait_recv()
    mortars(0)
    speed = finish_round(round_3, speed, cuts + ys - 2)
    step = 0.005 / jnp.broadcast_to(jnp.max(speed, keepdims=True), (8, LANES))
    scale = -(metric * step)
    scale = jnp.concatenate([scale] * 4, axis=0)

    def first_update(i, carry):
        rows = pl.ds(pl.multiple_of(i * 32, 32), 32)
        for v in range(NVAR):
            change = scale * rate[v, rows, :]
            reg_ref[v, rows, :] = change
            sect[v, rows, :] = u_ref[v, rows, :] + section_b[0] * change
        return carry

    lax.fori_loop(0, 16, first_update, 0)

    z_traces(sect, 1)
    zc = z_copies(1)
    for copy in zc:
        copy.start()
    send_mortars(sect, 1)
    mc = mortar_copies(1)
    for copy in mc:
        copy.start()
    started += zc + mc
    own_interpolated(sect)
    primitive_pass(sect, False)
    volume(sect)
    x_faces(sect)
    for copy in zc:
        copy.wait_recv()
    z_faces(1)
    for copy in mc:
        copy.wait_recv()
    mortars(1)

    def second_update(i, carry):
        rows = pl.ds(pl.multiple_of(i * 32, 32), 32)
        for v in range(NVAR):
            register = section_a[1] * reg_ref[v, rows, :] + scale * rate[v, rows, :]
            reg_ref[v, rows, :] = register
            adv_ref[v, rows, :] = sect[v, rows, :] + section_b[1] * register
        return carry

    lax.fori_loop(0, 16, second_update, 0)
    for copy in started:
        copy.wait_send()


def on_device(
    slabs, cuts, ys, zs,
    conserved,
    refinement,
    x_neighbour,
    coarse_element,
    quadrant,
    send_count,
    fine_element,
    orientation,
    receive_count,
):
    slots = jnp.arange(CAP, dtype=jnp.int32)[None, :]
    coarse_live = (slots < send_count.reshape(OFFS, 1)).astype(jnp.int32)
    fine_live = (slots < receive_count.reshape(OFFS, 1)).astype(jnp.int32)
    ints = jnp.stack([
        row.reshape(LANES)
        for row in (
            refinement, x_neighbour, coarse_element, quadrant,
            fine_element, orientation, coarse_live, fine_live,
        )
    ])
    peers = cuts + ys + zs - 3
    state = (NVAR, NP * FACE, LANES)
    face = (NVAR, FACE, LANES)
    return pl.pallas_call(
        functools.partial(kernel, slabs, cuts, ys, zs),
        out_shape=[jax.ShapeDtypeStruct(state, jnp.float32)] * 2,
        in_specs=[pl.BlockSpec(memory_space=pltpu.VMEM)] * 2,
        out_specs=[pl.BlockSpec(memory_space=pltpu.VMEM)] * 2,
        scratch_shapes=[
            pltpu.VMEM((4, NP * FACE, LANES), jnp.float32),
            pltpu.VMEM(state, jnp.float32),
            pltpu.VMEM(state, jnp.float32),
            pltpu.VMEM((2, 2) + face, jnp.float32),
            pltpu.VMEM((2, 2) + face, jnp.float32),
            pltpu.VMEM((2, OFFS, 24, LANES), jnp.float32),
            pltpu.VMEM((2, OFFS, 24, LANES), jnp.float32),
            pltpu.VMEM((2, OFFS, 80, LANES), jnp.float32),
            pltpu.VMEM((2, OFFS, 80, LANES), jnp.float32),
            pltpu.VMEM((3, 8, LANES), jnp.float32),
            pltpu.VMEM((peers, 8, LANES), jnp.float32),
            pltpu.VMEM(face, jnp.float32),
            pltpu.VMEM(face, jnp.float32),
            pltpu.VMEM(face, jnp.float32),
            pltpu.VMEM(face, jnp.float32),
            pltpu.VMEM(face, jnp.float32),
            pltpu.VMEM((12, 8, LANES), jnp.float32),
            pltpu.SemaphoreType.DMA((2, 2)),
            pltpu.SemaphoreType.DMA((2, 2)),
            pltpu.SemaphoreType.DMA((2, OFFS)),
            pltpu.SemaphoreType.DMA((2, OFFS)),
            pltpu.SemaphoreType.DMA((2, OFFS)),
            pltpu.SemaphoreType.DMA((2, OFFS)),
            pltpu.SemaphoreType.DMA((peers,)),
            pltpu.SemaphoreType.DMA((peers,)),
        ],
        compiler_params=pltpu.CompilerParams(
            collective_id=0, has_side_effects=True, vmem_limit_bytes=40 * 1024 * 1024
        ),
    )(conserved, ints)


def solution(mesh):
    slabs, cuts = mesh.shape["slab"], mesh.shape["cut"]
    zs = 12 if slabs % 12 == 0 else 3
    return jax.shard_map(
        functools.partial(on_device, slabs, cuts, slabs // zs, zs),
        mesh=mesh,
        in_specs=(
            P(None, None, ("slab", "cut")),
            P(("slab", "cut")),
            P(("slab", "cut"), None),
            P("slab", "cut", None, None),
            P("slab", "cut", None, None),
            P("slab", "cut", None),
            P("slab", "cut", None, None),
            P("slab", "cut", None, None),
            P("slab", "cut", None),
        ),
        out_specs=(P(None, None, ("slab", "cut")), P(None, None, ("slab", "cut"))),
        check_vma=False,
    )
```

time: 456 us -> 54.8 us (0.12)
  the two profiles are of different devices: /device:TPU:1 before, /device:TPU:8 now
where the time goes in v1:
time: 54.8 us; the launch traced here: 54.5 us
  Pallas kernels  45 us (82%)
  local copies, waits for them, and re-layouts  7.34 us (13%)
  other arithmetic  1.45 us (3%)
  between operations  0.65 us (1%)
    pallas_call x1, Pallas kernels, on_device(): pl.pallas_call(functools.partial(kernel, slabs, cuts, ys, zs), out_shape=...  45 us
    another operation x5, local copies, waits for them, and re-layouts, on_device(): jnp.stack([row.reshape(LANES) for row in (refinement, x_neighbour, coarse...  3.75 us
    unnamed x4, local copies, waits for them, and re-layouts  3.43 us

profile of v1, /device:TPU:8, one launch (start us, length us, event | category | flops | bytes accessed | tf_op | source)
XLA Modules:
  0.0 54.5 jit_solution(8422630751574501432)
XLA Ops:
  0.6 0.8 %stack_reshape.14 = s32[1,128]{1,0:T(1,128)S(1)} reshape(s32[1,1,4,32]{3,2,1,0:T(4,128)} %param.12) | data formatting | bytes 1024 | tf_op jit(solution)/shard_map/stack;reshape | solution.py:588
  1.4 0.8 %stack_reshape.15 = s32[1,128]{1,0:T(1,128)S(1)} reshape(s32[1,1,4,32]{3,2,1,0:T(4,128)} %param.13) | data formatting | bytes 1024 | tf_op jit(solution)/shard_map/stack;reshape | solution.py:588
  2.2 0.8 %stack_reshape.16 = s32[1,128]{1,0:T(1,128)S(1)} reshape(s32[1,1,4,32]{3,2,1,0:T(4,128)} %param.15) | data formatting | bytes 1024 | tf_op jit(solution)/shard_map/stack;reshape | solution.py:588
  2.9 0.8 %stack_reshape.17 = s32[1,128]{1,0:T(1,128)S(1)} reshape(s32[1,1,4,32]{3,2,1,0:T(4,128)} %param.16) | data formatting | bytes 1024 | tf_op jit(solution)/shard_map/stack;reshape | solution.py:588
  3.7 0.7 %fusion = s32[4,32]{1,0:T(4,128)S(1)} fusion(s32[4]{0:T(128)} %bitcast.3), kind=kLoop, calls=%fused_computation.2 | loop fusion | flops 256 | bytes 528 | tf_op jit(solution)/shard_map/convert_element_type | solution.py:586
  4.4 0.1 reshape.62
  4.5 0.7 %fusion.1 = s32[4,32]{1,0:T(4,128)S(1)} fusion(s32[4]{0:T(128)} %bitcast.4), kind=kLoop, calls=%fused_computation.3 | loop fusion | flops 256 | bytes 528 | tf_op jit(solution)/shard_map/convert_element_type | solution.py:587
  5.2 0.1 reshape.63
  5.3 0.7 %stack.7.ints_ref = s32[8,128]{1,0:T(8,128)S(1)} concatenate(s32[1,128]{1,0:T(1,128)} %bitcast.5, s32[1,128]{1,0:T(1,128)} %param.11, s32[1,128]{1,0:T(1,128)S(1)} %stack_reshape.14, s32[1,128]{1,0:T(1,128)S(1)} %stack_reshape.15, s32[1,128]{1,0:T(1,128)S(1)} %stack_reshape.16, s32[1,128]{1,0:T(1,128)S(1)} %stack_reshape.17, s32[1,128]{1,0:T(1,128)S(1)} %reshape.62, ...), dimensions={0} | concatenate | bytes 8192 | tf_op jit(solution)/shard_map/stack | solution.py:588
  6.0 0.0 copy-start
  6.0 1.3 %copy-done = f32[5,512,128]{2,1,0:T(8,128)S(1)} copy-done((f32[5,512,128]{2,1,0:T(8,128)S(1)}, f32[5,512,128]{2,1,0:T(8,128)}, u32[]{:S(2)}) %copy-start) | copy-done | bytes 1310744
  7.3 45.0 %shard_map.104 = (f32[5,512,128]{2,1,0:T(8,128)S(1)}, f32[5,512,128]{2,1,0:T(8,128)S(1)}) custom-call(f32[5,512,128]{2,1,0:T(8,128)S(1)} %copy-done, s32[8,128]{1,0:T(8,128)S(1)} %stack.7.ints_ref), custom_call_target="tpu_custom_call" | custom-call | tf_op jit(solution)/shard_map/pallas_call | solution.py:598
  52.4 1.1 %copy.13 = f32[5,512,128]{2,1,0:T(8,128)} copy(f32[5,512,128]{2,1,0:T(8,128)S(1)} %get-tuple-element.4) | data formatting | bytes 2621440
  53.4 1.1 %copy.14 = f32[5,512,128]{2,1,0:T(8,128)} copy(f32[5,512,128]{2,1,0:T(8,128)S(1)} %get-tuple-element.5) | data formatting | bytes 2621440
Async XLA Ops:
  6.0 1.3 %copy-start = (f32[5,512,128]{2,1,0:T(8,128)S(1)}, f32[5,512,128]{2,1,0:T(8,128)}, u32[]{:S(2)}) copy-start(f32[5,512,128]{2,1,0:T(8,128)} %u_ref.1) | copy-start | bytes 3932164

commit v2 on v1

v2 whole, which is shorter than its diff:
```python
import functools

import jax
import jax.numpy as jnp
import numpy as np
from jax import lax
from jax.experimental import pallas as pl
from jax.experimental.pallas import tpu as pltpu
from jax.sharding import PartitionSpec as P

NP = 8
NVAR = 5
FACE = NP * NP
LANES = 128
OFFS = 4
CAP = 32
UNROLL_SEND = NVAR
UNROLL_OWN = NVAR
UNROLL_EXPAND = NVAR
UNROLL_SCATTER = NVAR
UNROLL_FACE = 4
UNROLL_VOLUME = 2
UNROLL_UPDATE = 4
MESH = pl.DeviceIdType.MESH

section_a = (0.0, -567301805773.0 / 1357537059087.0)
section_b = (1432997174477.0 / 9575080441755.0, 5161836677717.0 / 13612068292357.0)


def legendre_rows(points, node_count):
    legendre = np.zeros((node_count, node_count))
    legendre[:, 0] = 1.0
    legendre[:, 1] = points
    for degree in range(2, node_count):
        legendre[:, degree] = (
            (2 * degree - 1) * points * legendre[:, degree - 1]
            - (degree - 1) * legendre[:, degree - 2]
        ) / degree
    return legendre


def lobatto(node_count):
    poly_order = node_count - 1
    points = -np.cos(np.pi * np.arange(node_count) / poly_order)
    for newton_step in range(40):
        legendre = legendre_rows(points, node_count)
        points = points - (points * legendre[:, poly_order] - legendre[:, poly_order - 1]) / (
            node_count * legendre[:, poly_order]
        )
    top_row = legendre_rows(points, node_count)[:, poly_order]
    weights = 2.0 / (poly_order * node_count * top_row * top_row)
    differ = np.zeros((node_count, node_count))
    for target in range(node_count):
        for source in range(node_count):
            if target != source:
                differ[target, source] = top_row[target] / (
                    top_row[source] * (points[target] - points[source])
                )
    differ[0, 0] = -poly_order * node_count / 4.0
    differ[poly_order, poly_order] = poly_order * node_count / 4.0
    lower_half = np.zeros((node_count, node_count))
    targets = (points - 1) / 2.0
    for source in range(node_count):
        basis = np.ones(node_count)
        for other in range(node_count):
            if other != source:
                basis = basis * (targets - points[other]) / (points[source] - points[other])
        lower_half[:, source] = basis
    lower_back = 0.5 * np.transpose(lower_half) * weights[None, :] / weights[:, None]
    return (weights, differ, lower_half, lower_back)


WEIGHTS, DIFFER, HALF, BACK = lobatto(NP)
LIFT = float(1.0 / WEIGHTS[0])
EVEN = 0.5 * (DIFFER[:4, :4] + DIFFER[:4, :3:-1])
ODD = 0.5 * (DIFFER[:4, :4] - DIFFER[:4, :3:-1])


def combine(row, values):
    total = None
    for weight, value in zip(row, values):
        weight = float(np.float32(weight))
        if abs(weight) < 1e-12:
            continue
        term = value if weight == 1.0 else weight * value
        total = term if total is None else total + term
    return total


def derive(f):
    even = [f[j] + f[7 - j] for j in range(4)]
    odd = [f[j] - f[7 - j] for j in range(4)]
    out = [None] * 8
    for i in range(4):
        from_even = combine(EVEN[i], even)
        from_odd = combine(ODD[i], odd)
        out[i] = from_odd + from_even
        out[7 - i] = from_odd - from_even
    return out


def half_map(matrix, upper, f):
    f = [jnp.where(upper, f[7 - j], f[j]) for j in range(8)]
    g = [combine(matrix[i], f) for i in range(8)]
    return [jnp.where(upper, g[7 - i], g[i]) for i in range(8)]


def primitives(u):
    inverse = 1.0 / u[0]
    velocity = [u[1] * inverse, u[2] * inverse, u[3] * inverse]
    carried = u[1] * velocity[0] + u[2] * velocity[1] + u[3] * velocity[2]
    pressure = 0.4 * (u[4] - 0.5 * carried)
    return inverse, velocity, pressure


def flux_of(u, normal, pressure, direction):
    rows = [u[1 + direction]]
    for column in range(3):
        carried = u[1 + column] * normal
        rows.append(carried + pressure if column == direction else carried)
    rows.append(normal * (u[4] + pressure))
    return rows


def face_flux(u, direction):
    inverse, velocity, pressure = primitives(u)
    normal = velocity[direction]
    speed = jnp.abs(normal) + jnp.sqrt(1.4 * pressure * inverse)
    return flux_of(u, normal, pressure, direction), speed


def face_parts(left, right, direction):
    left_flux, left_speed = face_flux(left, direction)
    right_flux, right_speed = face_flux(right, direction)
    half_speed = 0.5 * jnp.maximum(left_speed, right_speed)
    mean = [0.5 * (r - l) for l, r in zip(left_flux, right_flux)]
    jump = [half_speed * (r - l) for l, r in zip(left, right)]
    return mean, jump


def lane_pick(x, index):
    return jnp.take_along_axis(x, index, axis=1, mode="promise_in_bounds")


def swap_blocks(x, lane):
    high = lane >= 64
    odd = (lane // 32) % 2 == 1
    y = list(x)
    for k in (0, 1):
        y[k] = jnp.where(high, pltpu.roll(x[k + 2], 64, 1), x[k])
        y[k + 2] = jnp.where(high, x[k + 2], pltpu.roll(x[k], 64, 1))
    z = list(y)
    for k in (0, 2):
        z[k] = jnp.where(odd, pltpu.roll(y[k + 1], 32, 1), y[k])
        z[k + 1] = jnp.where(odd, y[k + 1], pltpu.roll(y[k], 96, 1))
    return z


def offset_distance(offset_index):
    return (offset_index // 2 + 1) * (1 - 2 * (offset_index % 2))


def eight(row):
    return jnp.broadcast_to(row, (8, LANES))


def tile(i):
    return pl.ds(pl.multiple_of(i * 8, 8), 8)


def loop(count, body, unroll):
    def step(i, carry):
        body(i)
        return carry

    lax.fori_loop(0, count, step, 0, unroll=unroll)


def kernel(
    slabs, cuts, ys, zs,
    u_hbm, ints_ref,
    adv_ref, reg_ref,
    u,
    prim, rate, sect,
    zsend, zrecv, csend, crecv, fsend, frecv,
    vsend, vrecv,
    own_coarse, own_fine, far_coarse, far_fine, coarse_term, fine_term, work, packed,
    in_sem, zs_sem, zr_sem, cs_sem, cr_sem, fs_sem, fr_sem, vs_sem, vr_sem,
):
    s = lax.axis_index("slab")
    t = lax.axis_index("cut")
    y = s // zs
    z = s % zs
    cut_peers = [(s, (t + d) % cuts) for d in range(1, cuts)]
    y_peers = [(((y + d) % ys) * zs + z, t) for d in range(1, ys)]
    z_peers = [(y * zs + (z + d) % zs, t) for d in range(1, zs)]
    ahead = [((s + offset_distance(o) + slabs) % slabs, t) for o in range(OFFS)]
    back = [((s - offset_distance(o) + slabs) % slabs, t) for o in range(OFFS)]

    loads = [
        pltpu.make_async_copy(
            u_hbm.at[:, pl.ds(64 * a, 64), :], u.at[:, pl.ds(64 * a, 64), :], in_sem.at[a]
        )
        for a in range(8)
    ]
    for copy in loads:
        copy.start()

    barrier = pltpu.get_barrier_semaphore()
    greeted = cut_peers + y_peers + z_peers + ahead
    for peer in greeted:
        pl.semaphore_signal(barrier, inc=1, device_id=peer, device_id_type=MESH)

    lane = lax.broadcasted_iota(jnp.int32, (8, LANES), 1)
    sub = lax.broadcasted_iota(jnp.int32, (8, LANES), 0)
    flipped = 7 - sub
    block = lane // CAP
    spread = lax.broadcasted_iota(jnp.int32, (LANES, LANES), 0)
    counting = (lane + 1).astype(jnp.float32)

    level = eight(ints_ref[0:1])
    metric = jnp.where(level == 0, 1.0, jnp.where(level == 1, 2.0, 4.0))
    negative = -metric

    fastest = jnp.zeros((32, LANES), jnp.float32)
    for a in range(8):
        loads[a].wait()

        def one(i, fastest):
            rows = pl.ds(pl.multiple_of(64 * a + i * 32, 32), 32)
            state = [u[v, rows, :] for v in range(NVAR)]
            inverse, velocity, pressure = primitives(state)
            for d in range(3):
                prim[d, rows, :] = velocity[d]
            prim[3, rows, :] = pressure
            square = velocity[0] * velocity[0] + velocity[1] * velocity[1] + velocity[2] * velocity[2]
            return jnp.maximum(fastest, jnp.sqrt(square) + jnp.sqrt(1.4 * pressure * inverse))

        fastest = lax.fori_loop(0, 2, one, fastest, unroll=True)
    speed = jnp.maximum(jnp.maximum(fastest[0:8], fastest[8:16]), jnp.maximum(fastest[16:24], fastest[24:32]))
    speed = jnp.max(speed * metric, axis=0, keepdims=True)
    vsend[0, 0:1] = speed

    def speed_round(number, first, peers):
        return [
            pltpu.make_async_remote_copy(
                src_ref=vsend.at[number, pl.ds(0, 1)], dst_ref=vrecv.at[first + i, pl.ds(0, 1)],
                send_sem=vs_sem.at[first + i], recv_sem=vr_sem.at[first + i],
                device_id=peer, device_id_type=MESH)
            for i, peer in enumerate(peers)
        ]

    def finish_round(copies, value, first):
        for copy in copies:
            copy.wait_recv()
        for i in range(len(copies)):
            value = jnp.maximum(value, vrecv[first + i, 0:1])
        return value

    round_1 = speed_round(0, 0, cut_peers)
    round_2 = speed_round(1, cuts - 1, y_peers)
    round_3 = speed_round(2, cuts + ys - 2, z_peers)

    def z_copies(stage):
        targets = [(s, (t + 1) % cuts), (s, (t + cuts - 1) % cuts)]
        return [
            pltpu.make_async_remote_copy(
                src_ref=zsend.at[stage, i], dst_ref=zrecv.at[stage, i],
                send_sem=zs_sem.at[stage, i], recv_sem=zr_sem.at[stage, i],
                device_id=targets[i], device_id_type=MESH)
            for i in range(2)
        ]

    def fine_copies(stage):
        return [
            pltpu.make_async_remote_copy(
                src_ref=fsend.at[stage, o], dst_ref=frecv.at[stage, o],
                send_sem=fs_sem.at[stage, o], recv_sem=fr_sem.at[stage, o],
                device_id=back[o], device_id_type=MESH)
            for o in range(OFFS)
        ]

    def coarse_copies(stage):
        return [
            pltpu.make_async_remote_copy(
                src_ref=csend.at[stage, o], dst_ref=crecv.at[stage, o],
                send_sem=cs_sem.at[stage, o], recv_sem=cr_sem.at[stage, o],
                device_id=ahead[o], device_id_type=MESH)
            for o in range(OFFS)
        ]

    pl.semaphore_wait(barrier, len(greeted))
    for copy in round_1:
        copy.start()

    def z_traces(read, stage):
        for v in range(NVAR):
            zsend[stage, 0, v] = read(v, pl.ds(7, FACE, stride=8))
            zsend[stage, 1, v] = read(v, pl.ds(0, FACE, stride=8))

    def read_state(v, rows):
        return u[v, rows, :]

    def read_rate(v, rows):
        values = rate[v, rows, :]
        return jnp.broadcast_to(negative[0:1], values.shape) * values

    z_first = z_copies(0)
    z_traces(read_state, 0)
    for copy in z_first:
        copy.start()

    def row_of(first):
        parts = [ints_ref[first + o : first + o + 1, 0:CAP] for o in range(OFFS)]
        return eight(jnp.concatenate(parts, axis=1))

    def live_of(row):
        count = jnp.broadcast_to(ints_ref[row : row + 1, 0:1], (8, LANES))
        for o in range(1, OFFS):
            count = jnp.where(block == o, jnp.broadcast_to(ints_ref[row : row + 1, o : o + 1], (8, LANES)), count)
        return lane % CAP < count

    neighbour = eight(ints_ref[8:9])
    coarse_index = row_of(16)
    quadrant = row_of(24)
    fine_index = row_of(32)
    turns = row_of(40)
    coarse_live = live_of(48)
    fine_live = live_of(56)
    own_a = quadrant >= 2
    own_c = quadrant % 2 == 1
    back_turns = (4 - turns) % 4
    group_pick = block * CAP + (lane % 8) * 4
    group_index = lane_pick(coarse_index, group_pick)
    group_block = (lane // 8) % 4
    widen = [block * CAP + k * 8 + (lane % CAP) // 4 for k in range(4)]

    def rev(x):
        return jnp.take_along_axis(x, flipped, axis=0, mode="promise_in_bounds")

    def rotated(read, amount):
        odd = amount % 2 == 1
        far = amount >= 2
        mixed = [
            jnp.where(odd, read(pl.ds(7 - i, 8, stride=8)), read(pl.ds(8 * i, 8)))
            for i in range(8)
        ]
        return [jnp.where(far, rev(mixed[7 - i]), mixed[i]) for i in range(8)]

    def half_both(matrix, upper_a, upper_c, values, v):
        along_a = half_map(matrix, upper_a, values)
        for i in range(8):
            work[v, pl.ds(8 * i, 8), :] = along_a[i]
        columns = [work[v, pl.ds(j, 8, stride=8), :] for j in range(8)]
        return half_map(matrix, upper_c, columns)

    def send_mortars(read, stage, fine, coarse):
        def fine_side(v):
            for a in range(8):
                work[v, pl.ds(8 * a, 8), :] = lane_pick(read(v, pl.ds(64 * a, 8)), fine_index)
            turned = rotated(lambda rows: work[v, rows, :], back_turns)
            for a in range(8):
                own_fine[stage, v, pl.ds(8 * a, 8), :] = turned[a]
            for h in range(2):
                blocks = swap_blocks(turned[4 * h : 4 * h + 4], lane)
                for o in range(OFFS):
                    fsend[stage, o, tile(2 * v + h), :] = blocks[o]

        loop(NVAR, fine_side, UNROLL_SEND)
        for copy in fine:
            copy.start()

        def coarse_side(v):
            for h in range(2):
                pack = lane_pick(read(v, pl.ds(256 * h + 56, 8)), group_index)
                for k in range(1, 4):
                    top = read(v, pl.ds(256 * h + 64 * k + 56, 8))
                    pack = jnp.where(group_block == k, lane_pick(top, group_index), pack)
                packed[2 * v + h] = pack

        loop(NVAR, coarse_side, UNROLL_SEND)
        packed[10] = quadrant.astype(jnp.float32)
        packed[11] = jnp.zeros((8, LANES), jnp.float32)
        for m in range(3):
            blocks = swap_blocks([packed[4 * m + k] for k in range(4)], lane)
            for o in range(OFFS):
                csend[stage, o, pl.ds(8 * m, 8), :] = blocks[o]
        for copy in coarse:
            copy.start()

    def own_interpolated(read, stage):
        def one(v):
            picked = [lane_pick(read(v, pl.ds(64 * a + 56, 8)), coarse_index) for a in range(8)]
            columns = half_both(HALF, own_a, own_c, picked, v)
            for j in range(8):
                own_coarse[stage, v, pl.ds(j, 8, stride=8), :] = columns[j]

        loop(NVAR, one, UNROLL_OWN)

    def line(read, normal, pressure, direction, v):
        if v == 0:
            return [read(1 + direction, j) for j in range(8)]
        if v == 4:
            return [normal[j] * (read(4, j) + pressure[j]) for j in range(8)]
        if v == 1 + direction:
            return [read(v, j) * normal[j] + pressure[j] for j in range(8)]
        return [read(v, j) * normal[j] for j in range(8)]

    def volume(state, direction, at, fresh):
        def one(i):
            normal = [prim[direction, at(i, j), :] for j in range(8)]
            pressure = [prim[3, at(i, j), :] for j in range(8)]
            for v in range(NVAR):
                out = derive(line(lambda w, j: state[w, at(i, j), :], normal, pressure, direction, v))
                for j in range(8):
                    if fresh:
                        rate[v, at(i, j), :] = out[j]
                    else:
                        rate[v, at(i, j), :] += out[j]

        loop(8, one, UNROLL_VOLUME)

    def volume_z(state):
        volume(state, 2, lambda a, j: pl.ds(a * 64 + j, 8, stride=8), True)

    def volume_y(state):
        volume(state, 1, lambda a, j: pl.ds(pl.multiple_of(a * 64 + j * 8, 8), 8), False)

    def volume_x(state):
        volume(state, 0, lambda b, j: pl.ds(pl.multiple_of(b * 8 + j * 64, 8), 8), False)

    def inverse_of(row, counts):
        table = jnp.where(spread == row, 1.0, 0.0).astype(jnp.bfloat16)
        found = lax.dot_general(
            counts.astype(jnp.bfloat16), table, (((1,), (1,)), ((), ())),
            preferred_element_type=jnp.float32,
        )
        present = found > 0.5
        return jnp.maximum(found - 1.0, 0.0).astype(jnp.int32), present

    x_source, _ = inverse_of(neighbour[0:1], counting)
    c_source, c_present = inverse_of(coarse_index[0:1], jnp.where(lane % 4 == 0, counting, 0.0))
    f_source, f_present = inverse_of(fine_index[0:1], counting)

    def x_faces(state):
        def one(i):
            low = pl.ds(pl.multiple_of(i * 16, 16), 16)
            high = pl.ds(pl.multiple_of(448 + i * 16, 16), 16)
            pick = jnp.broadcast_to(neighbour[0:1], (16, LANES))
            source = jnp.broadcast_to(x_source[0:1], (16, LANES))
            left = [state[v, high, :] for v in range(NVAR)]
            right = [lane_pick(state[v, low, :], pick) for v in range(NVAR)]
            mean, jump = face_parts(left, right, 0)
            for v in range(NVAR):
                rate[v, high, :] += LIFT * (mean[v] - jump[v])
                rate[v, low, :] += LIFT * lane_pick(mean[v] + jump[v], source)

        loop(4, one, UNROLL_FACE)

    def blend(ref, index, factor):
        if factor is None:
            return ref[(0,) + index]
        first = ref[(0,) + index]
        return first + jnp.broadcast_to(factor, first.shape) * ref[(1,) + index]

    def z_faces(factor):
        def one(i):
            rows = pl.ds(pl.multiple_of(i * 16, 16), 16)
            bottom = pl.ds(i * 128, 16, stride=8)
            top = pl.ds(i * 128 + 7, 16, stride=8)
            left = [blend(zsend, (0, v, rows, slice(None)), factor) for v in range(NVAR)]
            right = [blend(zrecv, (1, v, rows, slice(None)), factor) for v in range(NVAR)]
            mean, jump = face_parts(left, right, 2)
            for v in range(NVAR):
                rate[v, top, :] += LIFT * (mean[v] - jump[v])
            left = [blend(zrecv, (0, v, rows, slice(None)), factor) for v in range(NVAR)]
            right = [blend(zsend, (1, v, rows, slice(None)), factor) for v in range(NVAR)]
            mean, jump = face_parts(left, right, 2)
            for v in range(NVAR):
                rate[v, bottom, :] += LIFT * (mean[v] + jump[v])

        loop(4, one, UNROLL_FACE)

    def far_quadrants():
        far = packed[10]
        return far > 1.5, (far == 1.0) | (far == 3.0)

    def expand(stage):
        for m in range(3):
            blocks = swap_blocks([crecv[stage, o, pl.ds(8 * m, 8), :] for o in range(OFFS)], lane)
            for k in range(4):
                packed[4 * m + k] = blocks[k]
        far_a, far_c = far_quadrants()

        def one(v):
            for h in range(2):
                blocks = swap_blocks([frecv[stage, o, tile(2 * v + h), :] for o in range(OFFS)], lane)
                for k in range(4):
                    far_fine[stage, v, pl.ds(8 * (4 * h + k), 8), :] = blocks[k]
            picked = [lane_pick(packed[2 * v + a // 4], widen[a % 4]) for a in range(8)]
            columns = half_both(HALF, far_a, far_c, picked, v)
            for j in range(8):
                far_coarse[stage, v, pl.ds(j, 8, stride=8), :] = columns[j]

        loop(NVAR, one, UNROLL_EXPAND)

    def mortar_terms(factor):
        def fluxes(i):
            rows = pl.ds(pl.multiple_of(i * 16, 16), 16)
            live = jnp.concatenate([coarse_live, coarse_live], axis=0)
            left = [blend(own_coarse, (v, rows, slice(None)), factor) for v in range(NVAR)]
            right = [blend(far_fine, (v, rows, slice(None)), factor) for v in range(NVAR)]
            mean, jump = face_parts(left, right, 1)
            for v in range(NVAR):
                coarse_term[v, rows, :] = jnp.where(live, mean[v] - jump[v], 0.0)
            live = jnp.concatenate([fine_live, fine_live], axis=0)
            left = [blend(far_coarse, (v, rows, slice(None)), factor) for v in range(NVAR)]
            right = [blend(own_fine, (v, rows, slice(None)), factor) for v in range(NVAR)]
            mean, jump = face_parts(left, right, 1)
            for v in range(NVAR):
                fine_term[v, rows, :] = jnp.where(live, mean[v] + jump[v], 0.0)

        loop(4, fluxes, UNROLL_FACE)

        def scatter(v):
            values = [coarse_term[v, pl.ds(8 * a, 8), :] for a in range(8)]
            columns = half_both(BACK, own_a, own_c, values, v)
            for c in range(8):
                total = columns[c] + pltpu.roll(columns[c], 127, 1)
                total = total + pltpu.roll(total, 126, 1)
                share = jnp.where(c_present, lane_pick(total, c_source), 0.0)
                rate[v, pl.ds(56 + c, 8, stride=64), :] += LIFT * share
            turned = rotated(lambda rows: fine_term[v, rows, :], turns)
            for a in range(8):
                share = jnp.where(f_present, lane_pick(turned[a], f_source), 0.0)
                rate[v, pl.ds(64 * a, 8), :] += LIFT * share

        loop(NVAR, scatter, UNROLL_SCATTER)

    fine_first = fine_copies(0)
    coarse_first = coarse_copies(0)
    send_mortars(read_state, 0, fine_first, coarse_first)
    volume_z(u)
    volume_y(u)
    speed = finish_round(round_1, speed, 0)
    vsend[1, 0:1] = speed
    for copy in round_2:
        copy.start()
    volume_x(u)
    x_faces(u)
    own_interpolated(read_state, 0)
    for copy in z_first:
        copy.wait_recv()
    z_faces(None)
    speed = finish_round(round_2, speed, cuts - 1)
    vsend[2, 0:1] = speed
    for copy in round_3:
        copy.start()
    for copy in fine_first + coarse_first:
        copy.wait_recv()
    expand(0)
    mortar_terms(None)

    z_second = z_copies(1)
    z_traces(read_rate, 1)
    for copy in z_second:
        copy.start()
    fine_second = fine_copies(1)
    coarse_second = coarse_copies(1)
    send_mortars(read_rate, 1, fine_second, coarse_second)
    own_interpolated(read_rate, 1)
    speed = finish_round(round_3, speed, cuts + ys - 2)
    step = 0.005 / jnp.max(speed, axis=1, keepdims=True)
    scale = jnp.broadcast_to(negative[0:1] * step, (32, LANES))
    factor = section_b[0] * step

    def first_update(i):
        rows = pl.ds(pl.multiple_of(i * 32, 32), 32)
        state = []
        for v in range(NVAR):
            change = scale * rate[v, rows, :]
            reg_ref[v, rows, :] = change
            state.append(u[v, rows, :] + section_b[0] * change)
            sect[v, rows, :] = state[v]
        inverse, velocity, pressure = primitives(state)
        for d in range(3):
            prim[d, rows, :] = velocity[d]
        prim[3, rows, :] = pressure

    loop(16, first_update, UNROLL_UPDATE)

    volume_z(sect)
    volume_y(sect)
    volume_x(sect)
    x_faces(sect)
    for copy in z_second:
        copy.wait_recv()
    z_faces(factor)
    for copy in fine_second + coarse_second:
        copy.wait_recv()
    expand(1)
    mortar_terms(factor)

    def second_update(i):
        rows = pl.ds(pl.multiple_of(i * 32, 32), 32)
        for v in range(NVAR):
            register = section_a[1] * reg_ref[v, rows, :] + scale * rate[v, rows, :]
            reg_ref[v, rows, :] = register
            adv_ref[v, rows, :] = sect[v, rows, :] + section_b[1] * register

    loop(16, second_update, UNROLL_UPDATE)
    for copies in (round_1, round_2, round_3, z_first, z_second, fine_first, fine_second, coarse_first, coarse_second):
        for copy in copies:
            copy.wait_send()


def on_device(
    slabs, cuts, ys, zs,
    conserved,
    refinement,
    x_neighbour,
    coarse_element,
    quadrant,
    send_count,
    fine_element,
    orientation,
    receive_count,
):
    peers = cuts + ys + zs - 3
    state = (NVAR, NP * FACE, LANES)
    face = (NVAR, FACE, LANES)
    links = (OFFS, CAP)
    tables = (
        refinement.reshape(1, LANES), x_neighbour, coarse_element.reshape(links),
        quadrant.reshape(links), fine_element.reshape(links), orientation.reshape(links),
        send_count.reshape(1, OFFS), receive_count.reshape(1, OFFS),
    )
    ints = jnp.zeros((64, LANES), jnp.int32)
    for i, table in enumerate(tables):
        rows, columns = table.shape
        ints = jnp.maximum(ints, jnp.pad(table, ((8 * i, 64 - 8 * i - rows), (0, LANES - columns))))
    return pl.pallas_call(
        functools.partial(kernel, slabs, cuts, ys, zs),
        out_shape=[jax.ShapeDtypeStruct(state, jnp.float32)] * 2,
        in_specs=[pl.BlockSpec(memory_space=pltpu.HBM), pl.BlockSpec(memory_space=pltpu.VMEM)],
        out_specs=[pl.BlockSpec(memory_space=pltpu.VMEM)] * 2,
        scratch_shapes=[
            pltpu.VMEM(state, jnp.float32),
            pltpu.VMEM((4, NP * FACE, LANES), jnp.float32),
            pltpu.VMEM(state, jnp.float32),
            pltpu.VMEM(state, jnp.float32),
            pltpu.VMEM((2, 2) + face, jnp.float32),
            pltpu.VMEM((2, 2) + face, jnp.float32),
            pltpu.VMEM((2, OFFS, 24, LANES), jnp.float32),
            pltpu.VMEM((2, OFFS, 24, LANES), jnp.float32),
            pltpu.VMEM((2, OFFS, 80, LANES), jnp.float32),
            pltpu.VMEM((2, OFFS, 80, LANES), jnp.float32),
            pltpu.VMEM((3, 8, LANES), jnp.float32),
            pltpu.VMEM((peers, 8, LANES), jnp.float32),
            pltpu.VMEM((2,) + face, jnp.float32),
            pltpu.VMEM((2,) + face, jnp.float32),
            pltpu.VMEM((2,) + face, jnp.float32),
            pltpu.VMEM((2,) + face, jnp.float32),
            pltpu.VMEM(face, jnp.float32),
            pltpu.VMEM(face, jnp.float32),
            pltpu.VMEM(face, jnp.float32),
            pltpu.VMEM((12, 8, LANES), jnp.float32),
            pltpu.SemaphoreType.DMA((8,)),
            pltpu.SemaphoreType.DMA((2, 2)),
            pltpu.SemaphoreType.DMA((2, 2)),
            pltpu.SemaphoreType.DMA((2, OFFS)),
            pltpu.SemaphoreType.DMA((2, OFFS)),
            pltpu.SemaphoreType.DMA((2, OFFS)),
            pltpu.SemaphoreType.DMA((2, OFFS)),
            pltpu.SemaphoreType.DMA((peers,)),
            pltpu.SemaphoreType.DMA((peers,)),
        ],
        compiler_params=pltpu.CompilerParams(
            collective_id=0, has_side_effects=True, vmem_limit_bytes=51 * 1024 * 1024
        ),
    )(conserved, ints)


def solution(mesh):
    slabs, cuts = mesh.shape["slab"], mesh.shape["cut"]
    zs = 12 if slabs % 12 == 0 else 3
    return jax.shard_map(
        functools.partial(on_device, slabs, cuts, slabs // zs, zs),
        mesh=mesh,
        in_specs=(
            P(None, None, ("slab", "cut")),
            P(("slab", "cut")),
            P(("slab", "cut"), None),
            P("slab", "cut", None, None),
            P("slab", "cut", None, None),
            P("slab", "cut", None),
            P("slab", "cut", None, None),
            P("slab", "cut", None, None),
            P("slab", "cut", None),
        ),
        out_specs=(P(None, None, ("slab", "cut")), P(None, None, ("slab", "cut"))),
        check_vma=False,
    )
```

time: 54.8 us -> 41.7 us (0.76)
  the two profiles are of different devices: /device:TPU:8 before, /device:TPU:1 now
where the time goes in v2:
time: 41.7 us; the launch traced here: 41.5 us
  Pallas kernels  38 us (91%)
  local copies, waits for them, and re-layouts  2.11 us (5%)
  other arithmetic  0.79 us (2%)
  between operations  0.64 us (2%)
    pallas_call x1, Pallas kernels, on_device(): pl.pallas_call(functools.partial(kernel, slabs, cuts, ys, zs), out_shape=...  38 us
    unnamed x2, local copies, waits for them, and re-layouts  2.11 us

profile of v2, /device:TPU:1, one launch (start us, length us, event | category | flops | bytes accessed | tf_op | source)
XLA Modules:
  0.0 41.5 jit_solution(1247628035832801805)
XLA Ops:
  0.6 0.8 %pad_maximum_fusion.ints_ref = s32[64,128]{1,0:T(8,128)S(1)} fusion(s32[1,4]{1,0:T(1,128)} %bitcast.11, s32[1,4]{1,0:T(1,128)} %bitcast.12, s32[4,32]{1,0:T(4,128)} %bitcast.7, s32[4,32]{1,0:T(4,128)} %bitcast.8, s32[4,32]{1,0:T(4,128)} %bitcast.9, s32[4,32]{1,0:T(4,128)} %bitcast.10, s32[1,128]{1,0:T(1,128)} %param.11, s32[1,128]{1,0:T(1,128)} %bitcast.13), kind=kLoop, calls=%fused_computation | loop fusion | flops 65536 | bytes 35872 | tf_op jit(solution)/shard_map/max | solution.py:641
  1.4 38.0 %shard_map.104 = (f32[5,512,128]{2,1,0:T(8,128)S(1)}, f32[5,512,128]{2,1,0:T(8,128)S(1)}) custom-call(f32[5,512,128]{2,1,0:T(8,128)} %u_hbm.1, s32[64,128]{1,0:T(8,128)S(1)} %pad_maximum_fusion.ints_ref), custom_call_target="tpu_custom_call" | custom-call | tf_op jit(solution)/shard_map/pallas_call | solution.py:642
  39.4 1.1 %copy.13 = f32[5,512,128]{2,1,0:T(8,128)} copy(f32[5,512,128]{2,1,0:T(8,128)S(1)} %get-tuple-element.4) | data formatting | bytes 2621440
  40.5 1.1 %copy.14 = f32[5,512,128]{2,1,0:T(8,128)} copy(f32[5,512,128]{2,1,0:T(8,128)S(1)} %get-tuple-element.5) | data formatting | bytes 2621440

commit v3 on v2

--- a/solution.py
+++ b/solution.py
@@ -16,7 +16,7 @@
 CAP = 32
 UNROLL_SEND = NVAR
 UNROLL_OWN = NVAR
-UNROLL_EXPAND = NVAR
+UNROLL_EXPAND = 1
 UNROLL_SCATTER = NVAR
 UNROLL_FACE = 4
 UNROLL_VOLUME = 2
@@ -179,9 +179,9 @@
 def kernel(
     slabs, cuts, ys, zs,
     u_hbm, ints_ref,
-    adv_ref, reg_ref,
+    rate, reg_ref, sect, scale_ref,
     u,
-    prim, rate, sect,
+    prim,
     zsend, zrecv, csend, crecv, fsend, frecv,
     vsend, vrecv,
     own_coarse, own_fine, far_coarse, far_fine, coarse_term, fine_term, work, packed,
@@ -277,7 +277,7 @@
                 src_ref=fsend.at[stage, o], dst_ref=frecv.at[stage, o],
                 send_sem=fs_sem.at[stage, o], recv_sem=fr_sem.at[stage, o],
                 device_id=back[o], device_id_type=MESH)
-            for o in range(OFFS)
+            for o in (2, 3, 0, 1)
         ]
 
     def coarse_copies(stage):
@@ -286,7 +286,7 @@
                 src_ref=csend.at[stage, o], dst_ref=crecv.at[stage, o],
                 send_sem=cs_sem.at[stage, o], recv_sem=cr_sem.at[stage, o],
                 device_id=ahead[o], device_id_type=MESH)
-            for o in range(OFFS)
+            for o in (2, 3, 0, 1)
         ]
 
     pl.semaphore_wait(barrier, len(greeted))
@@ -304,11 +304,6 @@
     def read_rate(v, rows):
         values = rate[v, rows, :]
         return jnp.broadcast_to(negative[0:1], values.shape) * values
-
-    z_first = z_copies(0)
-    z_traces(read_state, 0)
-    for copy in z_first:
-        copy.start()
 
     def row_of(first):
         parts = [ints_ref[first + o : first + o + 1, 0:CAP] for o in range(OFFS)]
@@ -540,6 +535,10 @@
     fine_first = fine_copies(0)
     coarse_first = coarse_copies(0)
     send_mortars(read_state, 0, fine_first, coarse_first)
+    z_first = z_copies(0)
+    z_traces(read_state, 0)
+    for copy in z_first:
+        copy.start()
     volume_z(u)
     volume_y(u)
     speed = finish_round(round_1, speed, 0)
@@ -549,9 +548,6 @@
     volume_x(u)
     x_faces(u)
     own_interpolated(read_state, 0)
-    for copy in z_first:
-        copy.wait_recv()
-    z_faces(None)
     speed = finish_round(round_2, speed, cuts - 1)
     vsend[2, 0:1] = speed
     for copy in round_3:
@@ -560,26 +556,30 @@
         copy.wait_recv()
     expand(0)
     mortar_terms(None)
-
+    for copy in z_first:
+        copy.wait_recv()
+    z_faces(None)
+
+    fine_second = fine_copies(1)
+    coarse_second = coarse_copies(1)
+    send_mortars(read_rate, 1, fine_second, coarse_second)
     z_second = z_copies(1)
     z_traces(read_rate, 1)
     for copy in z_second:
         copy.start()
-    fine_second = fine_copies(1)
-    coarse_second = coarse_copies(1)
-    send_mortars(read_rate, 1, fine_second, coarse_second)
     own_interpolated(read_rate, 1)
     speed = finish_round(round_3, speed, cuts + ys - 2)
     step = 0.005 / jnp.max(speed, axis=1, keepdims=True)
     scale = jnp.broadcast_to(negative[0:1] * step, (32, LANES))
     factor = section_b[0] * step
+    scale_ref[...] = scale[0:8]
 
     def first_update(i):
         rows = pl.ds(pl.multiple_of(i * 32, 32), 32)
         state = []
         for v in range(NVAR):
             change = scale * rate[v, rows, :]
-            reg_ref[v, rows, :] = change
+            reg_ref[v, rows, :] = section_a[1] * change
             state.append(u[v, rows, :] + section_b[0] * change)
             sect[v, rows, :] = state[v]
         inverse, velocity, pressure = primitives(state)
@@ -593,22 +593,14 @@
     volume_y(sect)
     volume_x(sect)
     x_faces(sect)
-    for copy in z_second:
-        copy.wait_recv()
-    z_faces(factor)
     for copy in fine_second + coarse_second:
         copy.wait_recv()
     expand(1)
     mortar_terms(factor)
-
-    def second_update(i):
-        rows = pl.ds(pl.multiple_of(i * 32, 32), 32)
-        for v in range(NVAR):
-            register = section_a[1] * reg_ref[v, rows, :] + scale * rate[v, rows, :]
-            reg_ref[v, rows, :] = register
-            adv_ref[v, rows, :] = sect[v, rows, :] + section_b[1] * register
-
-    loop(16, second_update, UNROLL_UPDATE)
+    for copy in z_second:
+        copy.wait_recv()
+    z_faces(factor)
+
     for copies in (round_1, round_2, round_3, z_first, z_second, fine_first, fine_second, coarse_first, coarse_second):
         for copy in copies:
             copy.wait_send()
@@ -639,16 +631,15 @@
     for i, table in enumerate(tables):
         rows, columns = table.shape
         ints = jnp.maximum(ints, jnp.pad(table, ((8 * i, 64 - 8 * i - rows), (0, LANES - columns))))
-    return pl.pallas_call(
+    rate, before, sectioned, scale = pl.pallas_call(
         functools.partial(kernel, slabs, cuts, ys, zs),
-        out_shape=[jax.ShapeDtypeStruct(state, jnp.float32)] * 2,
+        out_shape=[jax.ShapeDtypeStruct(state, jnp.float32)] * 3
+        + [jax.ShapeDtypeStruct((8, LANES), jnp.float32)],
         in_specs=[pl.BlockSpec(memory_space=pltpu.HBM), pl.BlockSpec(memory_space=pltpu.VMEM)],
-        out_specs=[pl.BlockSpec(memory_space=pltpu.VMEM)] * 2,
+        out_specs=[pl.BlockSpec(memory_space=pltpu.VMEM)] * 4,
         scratch_shapes=[
             pltpu.VMEM(state, jnp.float32),
             pltpu.VMEM((4, NP * FACE, LANES), jnp.float32),
-            pltpu.VMEM(state, jnp.float32),
-            pltpu.VMEM(state, jnp.float32),
             pltpu.VMEM((2, 2) + face, jnp.float32),
             pltpu.VMEM((2, 2) + face, jnp.float32),
             pltpu.VMEM((2, OFFS, 24, LANES), jnp.float32),
@@ -676,9 +667,11 @@
             pltpu.SemaphoreType.DMA((peers,)),
         ],
         compiler_params=pltpu.CompilerParams(
-            collective_id=0, has_side_effects=True, vmem_limit_bytes=51 * 1024 * 1024
+            collective_id=0, has_side_effects=True, vmem_limit_bytes=50 * 1024 * 1024
         ),
     )(conserved, ints)
+    register = before + scale[0] * rate
+    return sectioned + section_b[1] * register, register
 
 
 def solution(mesh):

time: 41.7 us -> 41.6 us (level)
  local copies, waits for them, and re-layouts: 2.11 us -> 0.01 us
  other arithmetic: 0.79 us -> 2.5 us
    unnamed x2 -> x0, local copies, waits for them, and re-layouts: 2.11 us -> none
    add x0 -> x1, other arithmetic: none -> 1.71 us  [on_device(): return (sectioned + section_b[1] * register, register)]
where the time goes in v3:
time: 41.6 us; the launch traced here: 41.4 us
  Pallas kernels  38.3 us (92%)
  other arithmetic  2.5 us (6%)
  between operations  0.65 us (2%)
    pallas_call x1, Pallas kernels, on_device(): pl.pallas_call(functools.partial(kernel, slabs, cuts, ys, zs), out_shape=...  38.3 us
    add x1, other arithmetic, on_device(): return (sectioned + section_b[1] * register, register)  1.71 us

profile of v3, /device:TPU:1, one launch (start us, length us, event | category | flops | bytes accessed | tf_op | source)
XLA Modules:
  0.0 41.4 jit_solution(12718096141734128208)
XLA Ops:
  0.6 0.8 %pad_maximum_fusion.ints_ref = s32[64,128]{1,0:T(8,128)S(1)} fusion(s32[1,4]{1,0:T(1,128)} %bitcast.13, s32[1,4]{1,0:T(1,128)} %bitcast.14, s32[4,32]{1,0:T(4,128)} %bitcast.9, s32[4,32]{1,0:T(4,128)} %bitcast.10, s32[4,32]{1,0:T(4,128)} %bitcast.11, s32[4,32]{1,0:T(4,128)} %bitcast.12, s32[1,128]{1,0:T(1,128)} %param.11, s32[1,128]{1,0:T(1,128)} %bitcast.15), kind=kLoop, calls=%fused_computation.2 | loop fusion | flops 65536 | bytes 35872 | tf_op jit(solution)/shard_map/max | solution.py:633
  1.4 38.3 %shard_map.104 = (f32[5,512,128]{2,1,0:T(8,128)S(1)}, f32[5,512,128]{2,1,0:T(8,128)S(1)}, f32[5,512,128]{2,1,0:T(8,128)S(1)}, f32[8,128]{1,0:T(8,128)S(1)}) custom-call(f32[5,512,128]{2,1,0:T(8,128)} %u_hbm.1, s32[64,128]{1,0:T(8,128)S(1)} %pad_maximum_fusion.ints_ref), custom_call_target="tpu_custom_call" | custom-call | tf_op jit(solution)/shard_map/pallas_call | solution.py:634
  39.7 1.7 %multiply_add_fusion = (f32[5,512,128]{2,1,0:T(8,128)}, f32[5,512,128]{2,1,0:T(8,128)}) fusion(f32[5,512,128]{2,1,0:T(8,128)S(1)} %get-tuple-element.6, f32[5,512,128]{2,1,0:T(8,128)S(1)} %get-tuple-element.7, f32[5,512,128]{2,1,0:T(8,128)S(1)} %get-tuple-element.9, f32[128]{0:T(128)S(1)} %slice_bitcast_fusion), kind=kLoop, calls=%fused_computation | loop fusion | flops 1310720 | bytes 6554112 | tf_op jit(solution)/shard_map/add | solution.py:674
  (1 shorter events, 0.0 us)

commit v4 on v3

--- a/solution.py
+++ b/solution.py
@@ -179,9 +179,9 @@
 def kernel(
     slabs, cuts, ys, zs,
     u_hbm, ints_ref,
-    rate, reg_ref, sect, scale_ref,
+    rate_1, rate_2, sect, scale_ref,
     u,
-    prim,
+    prim, density_1, density_2,
     zsend, zrecv, csend, crecv, fsend, frecv,
     vsend, vrecv,
     own_coarse, own_fine, far_coarse, far_fine, coarse_term, fine_term, work, packed,
@@ -302,7 +302,7 @@
         return u[v, rows, :]
 
     def read_rate(v, rows):
-        values = rate[v, rows, :]
+        values = rate_1[v, rows, :]
         return jnp.broadcast_to(negative[0:1], values.shape) * values
 
     def row_of(first):
@@ -392,6 +392,8 @@
 
         loop(NVAR, one, UNROLL_OWN)
 
+    total_rate = [rate_1]
+
     def line(read, normal, pressure, direction, v):
         if v == 0:
             return [read(1 + direction, j) for j in range(8)]
@@ -402,27 +404,49 @@
         return [read(v, j) * normal[j] for j in range(8)]
 
     def volume(state, direction, at, fresh):
+        first = state is u
+
         def one(i):
             normal = [prim[direction, at(i, j), :] for j in range(8)]
             pressure = [prim[3, at(i, j), :] for j in range(8)]
-            for v in range(NVAR):
+            for v in range(0 if first else 1, NVAR):
                 out = derive(line(lambda w, j: state[w, at(i, j), :], normal, pressure, direction, v))
                 for j in range(8):
-                    if fresh:
-                        rate[v, at(i, j), :] = out[j]
-                    else:
-                        rate[v, at(i, j), :] += out[j]
+                    total = out[j] if fresh else total_rate[0][v, at(i, j), :] + out[j]
+                    total_rate[0][v, at(i, j), :] = total
+                    if v == 0 and direction == 0:
+                        density_1[at(i, j), :] = total
 
         loop(8, one, UNROLL_VOLUME)
 
+    def density_of_rate(direction, at, fresh):
+        def one(i):
+            out = derive([rate_1[1 + direction, at(i, j), :] for j in range(8)])
+            for j in range(8):
+                if fresh:
+                    density_2[at(i, j), :] = out[j]
+                else:
+                    density_2[at(i, j), :] += out[j]
+
+        loop(8, one, UNROLL_VOLUME)
+
+    def lines_z(a, j):
+        return pl.ds(a * 64 + j, 8, stride=8)
+
+    def lines_y(a, j):
+        return pl.ds(pl.multiple_of(a * 64 + j * 8, 8), 8)
+
+    def lines_x(b, j):
+        return pl.ds(pl.multiple_of(b * 8 + j * 64, 8), 8)
+
     def volume_z(state):
-        volume(state, 2, lambda a, j: pl.ds(a * 64 + j, 8, stride=8), True)
+        volume(state, 2, lines_z, True)
 
     def volume_y(state):
-        volume(state, 1, lambda a, j: pl.ds(pl.multiple_of(a * 64 + j * 8, 8), 8), False)
+        volume(state, 1, lines_y, False)
 
     def volume_x(state):
-        volume(state, 0, lambda b, j: pl.ds(pl.multiple_of(b * 8 + j * 64, 8), 8), False)
+        volume(state, 0, lines_x, False)
 
     def inverse_of(row, counts):
         table = jnp.where(spread == row, 1.0, 0.0).astype(jnp.bfloat16)
@@ -447,8 +471,8 @@
             right = [lane_pick(state[v, low, :], pick) for v in range(NVAR)]
             mean, jump = face_parts(left, right, 0)
             for v in range(NVAR):
-                rate[v, high, :] += LIFT * (mean[v] - jump[v])
-                rate[v, low, :] += LIFT * lane_pick(mean[v] + jump[v], source)
+                total_rate[0][v, high, :] += LIFT * (mean[v] - jump[v])
+                total_rate[0][v, low, :] += LIFT * lane_pick(mean[v] + jump[v], source)
 
         loop(4, one, UNROLL_FACE)
 
@@ -467,12 +491,12 @@
             right = [blend(zrecv, (1, v, rows, slice(None)), factor) for v in range(NVAR)]
             mean, jump = face_parts(left, right, 2)
             for v in range(NVAR):
-                rate[v, top, :] += LIFT * (mean[v] - jump[v])
+                total_rate[0][v, top, :] += LIFT * (mean[v] - jump[v])
             left = [blend(zrecv, (0, v, rows, slice(None)), factor) for v in range(NVAR)]
             right = [blend(zsend, (1, v, rows, slice(None)), factor) for v in range(NVAR)]
             mean, jump = face_parts(left, right, 2)
             for v in range(NVAR):
-                rate[v, bottom, :] += LIFT * (mean[v] + jump[v])
+                total_rate[0][v, bottom, :] += LIFT * (mean[v] + jump[v])
 
         loop(4, one, UNROLL_FACE)
 
@@ -524,11 +548,11 @@
                 total = columns[c] + pltpu.roll(columns[c], 127, 1)
                 total = total + pltpu.roll(total, 126, 1)
                 share = jnp.where(c_present, lane_pick(total, c_source), 0.0)
-                rate[v, pl.ds(56 + c, 8, stride=64), :] += LIFT * share
+                total_rate[0][v, pl.ds(56 + c, 8, stride=64), :] += LIFT * share
             turned = rotated(lambda rows: fine_term[v, rows, :], turns)
             for a in range(8):
                 share = jnp.where(f_present, lane_pick(turned[a], f_source), 0.0)
-                rate[v, pl.ds(64 * a, 8), :] += LIFT * share
+                total_rate[0][v, pl.ds(64 * a, 8), :] += LIFT * share
 
         loop(NVAR, scatter, UNROLL_SCATTER)
 
@@ -568,20 +592,23 @@
     for copy in z_second:
         copy.start()
     own_interpolated(read_rate, 1)
+    density_of_rate(2, lines_z, True)
+    density_of_rate(1, lines_y, False)
+    density_of_rate(0, lines_x, False)
     speed = finish_round(round_3, speed, cuts + ys - 2)
     step = 0.005 / jnp.max(speed, axis=1, keepdims=True)
     scale = jnp.broadcast_to(negative[0:1] * step, (32, LANES))
     factor = section_b[0] * step
     scale_ref[...] = scale[0:8]
+    blended = section_b[0] * scale
 
     def first_update(i):
         rows = pl.ds(pl.multiple_of(i * 32, 32), 32)
         state = []
         for v in range(NVAR):
-            change = scale * rate[v, rows, :]
-            reg_ref[v, rows, :] = section_a[1] * change
-            state.append(u[v, rows, :] + section_b[0] * change)
+            state.append(u[v, rows, :] + blended * rate_1[v, rows, :])
             sect[v, rows, :] = state[v]
+        rate_2[0, rows, :] = density_1[rows, :] + blended * density_2[rows, :]
         inverse, velocity, pressure = primitives(state)
         for d in range(3):
             prim[d, rows, :] = velocity[d]
@@ -589,6 +616,7 @@
 
     loop(16, first_update, UNROLL_UPDATE)
 
+    total_rate[0] = rate_2
     volume_z(sect)
     volume_y(sect)
     volume_x(sect)
@@ -631,7 +659,7 @@
     for i, table in enumerate(tables):
         rows, columns = table.shape
         ints = jnp.maximum(ints, jnp.pad(table, ((8 * i, 64 - 8 * i - rows), (0, LANES - columns))))
-    rate, before, sectioned, scale = pl.pallas_call(
+    rate_1, rate_2, sectioned, scale = pl.pallas_call(
         functools.partial(kernel, slabs, cuts, ys, zs),
         out_shape=[jax.ShapeDtypeStruct(state, jnp.float32)] * 3
         + [jax.ShapeDtypeStruct((8, LANES), jnp.float32)],
@@ -640,6 +668,8 @@
         scratch_shapes=[
             pltpu.VMEM(state, jnp.float32),
             pltpu.VMEM((4, NP * FACE, LANES), jnp.float32),
+            pltpu.VMEM((NP * FACE, LANES), jnp.float32),
+            pltpu.VMEM((NP * FACE, LANES), jnp.float32),
             pltpu.VMEM((2, 2) + face, jnp.float32),
             pltpu.VMEM((2, 2) + face, jnp.float32),
             pltpu.VMEM((2, OFFS, 24, LANES), jnp.float32),
@@ -670,7 +700,7 @@
             collective_id=0, has_side_effects=True, vmem_limit_bytes=50 * 1024 * 1024
         ),
     )(conserved, ints)
-    register = before + scale[0] * rate
+    register = scale[0] * (section_a[1] * rate_1 + rate_2)
     return sectioned + section_b[1] * register, register
 
 

time: 41.6 us -> 41.3 us (level)
  no operation moved by 1% of the time
where the time goes in v4:
time: 41.3 us; the launch traced here: 41.1 us
  Pallas kernels  38 us (92%)
  other arithmetic  2.54 us (6%)
  between operations  0.65 us (2%)
    pallas_call x1, Pallas kernels, on_device(): pl.pallas_call(functools.partial(kernel, slabs, cuts, ys, zs), out_shape=...  38 us
    add x1, other arithmetic, on_device(): return (sectioned + section_b[1] * register, register)  1.75 us

profile of v4, /device:TPU:1, one launch (start us, length us, event | category | flops | bytes accessed | tf_op | source)
XLA Modules:
  0.0 41.1 jit_solution(8975477551149591162)
XLA Ops:
  0.6 0.8 %pad_maximum_fusion.ints_ref = s32[64,128]{1,0:T(8,128)S(1)} fusion(s32[1,4]{1,0:T(1,128)} %bitcast.13, s32[1,4]{1,0:T(1,128)} %bitcast.14, s32[4,32]{1,0:T(4,128)} %bitcast.9, s32[4,32]{1,0:T(4,128)} %bitcast.10, s32[4,32]{1,0:T(4,128)} %bitcast.11, s32[4,32]{1,0:T(4,128)} %bitcast.12, s32[1,128]{1,0:T(1,128)} %param.11, s32[1,128]{1,0:T(1,128)} %bitcast.15), kind=kLoop, calls=%fused_computation.2 | loop fusion | flops 65536 | bytes 35872 | tf_op jit(solution)/shard_map/max | solution.py:661
  1.4 38.0 %shard_map.104 = (f32[5,512,128]{2,1,0:T(8,128)S(1)}, f32[5,512,128]{2,1,0:T(8,128)S(1)}, f32[5,512,128]{2,1,0:T(8,128)S(1)}, f32[8,128]{1,0:T(8,128)S(1)}) custom-call(f32[5,512,128]{2,1,0:T(8,128)} %u_hbm.1, s32[64,128]{1,0:T(8,128)S(1)} %pad_maximum_fusion.ints_ref), custom_call_target="tpu_custom_call" | custom-call | tf_op jit(solution)/shard_map/pallas_call | solution.py:662
  39.4 1.8 %multiply_add_fusion = (f32[5,512,128]{2,1,0:T(8,128)}, f32[5,512,128]{2,1,0:T(8,128)}) fusion(f32[5,512,128]{2,1,0:T(8,128)S(1)} %get-tuple-element.6, f32[5,512,128]{2,1,0:T(8,128)S(1)} %get-tuple-element.9, f32[5,512,128]{2,1,0:T(8,128)S(1)} %get-tuple-element.8, f32[128]{0:T(128)S(1)} %slice_bitcast_fusion), kind=kLoop, calls=%fused_computation | loop fusion | flops 1638400 | bytes 6554112 | tf_op jit(solution)/shard_map/add | solution.py:704
  (1 shorter events, 0.0 us)
